TPU v7x, 256 devices: a whole 4x4x8 slice. The times are simulated.
256 devices in a mesh: frame: 16 (over y, z_hi), row: 16 (over z_lo, x, core).
Axes of the slice: x: 4, y: 4, z: 8 (z_hi: 4, z_lo: 2; z = z_hi * 2 + z_lo), core: 2. Of those that a mesh axis runs over, the one named last changes fastest.
Arguments:
- frames_x: bfloat16 [16, 96, 128, 512], P('frame', 'row'), may hold values from -6 to 6
- conv_weight: bfloat16 [3, 3, 512, 512], replicated, may hold values from -0.09375 to 0.09375
- conv_bias: float32 [512], replicated, may hold values from -3 to 3
- query_weight: bfloat16 [512, 512], replicated, may hold values from -0.25 to 0.25
- key_weight: bfloat16 [512, 512], replicated, may hold values from -0.25 to 0.25
- value_weight: bfloat16 [512, 512], replicated, may hold values from -0.25 to 0.25
- out_weight: bfloat16 [512, 512], replicated, may hold values from -0.25 to 0.25
- query_gain: float32 [512], replicated, may hold values from 0.5 to 2
- key_gain: float32 [512], replicated, may hold values from 0.5 to 2
- source_ids: int32 [16, 96, 4], P('frame', 'row'), may hold values from 0 to 95, as said below
- valid_counts: int32 [16, 96], P('frame', 'row'), may hold values from 1 to 4
Outputs:
- propagated: bfloat16 [16, 96, 128, 512], P('frame', 'row')
Inputs may be any that keep to these rules, and one draw needn't show every extreme that they name: `source_ids`: block id s names row s // 1 of the previous frame, which lies at most 2 rows from the querying block's row; in every frame slot 0 of the blocks in even rows names a block 2 rows above and in odd rows 2 rows below, as far as the frame has that row.
All inputs are finite; a program needn't handle non-finite values.
Results may differ from a plain program's by a relative error of at most 0.0054.
Values may be sent and summed in bfloat16 or wider, within the bound.
No kernel may reach another device: no remote copies, remote signals or barrier semaphores. Data moves between devices by JAX's collectives and lax.ppermute only.
A program may use at most 64 MiB of HBM per device.

v0:
```python
import jax
import jax.numpy as jnp
from jax import lax
from jax.sharding import PartitionSpec as P

HEADS = 8
HD = 64
KSRC = 4
BLOCK = 128
DISP = 2


def with_halo(shard, sides, width):
    for axis, dim in sides:
        peers, length = (lax.axis_size(axis), shard.shape[dim])
        up = [(i, (i + 1) % peers) for i in range(peers - 1)]
        down = [(j, i) for i, j in up]
        last = lax.slice_in_dim(shard, length - width, length, axis=dim)
        initial = lax.slice_in_dim(shard, 0, width, axis=dim)
        before = lax.ppermute(last, axis, up)
        after = lax.ppermute(initial, axis, down)
        shard = jnp.concatenate([before, shard, after], axis=dim)
    return shard


def shifted(block, axis, distance):
    devices = range(lax.axis_size(axis))
    route = [(i - distance, i) for i in devices if i - distance in devices]
    return lax.ppermute(block, axis, route)


def normed(feats, weight, gain):
    proj = jnp.dot(feats, weight, preferred_element_type=jnp.float32).reshape(-1, HEADS, HD)
    proj = (
        proj
        * lax.rsqrt(jnp.mean(proj * proj, axis=-1, keepdims=True) + 1e-06)
        * gain.reshape(HEADS, HD)
    )
    return proj.reshape(-1, HEADS * HD).astype(jnp.bfloat16)


def shards(
    frames_x,
    conv_weight,
    conv_bias,
    query_weight,
    key_weight,
    value_weight,
    out_weight,
    query_gain,
    key_gain,
    source_ids,
    valid_counts,
):
    band_rows = frames_x.shape[1]
    width = frames_x.shape[2]
    chans = frames_x.shape[3]
    per_row = width // BLOCK
    tokens = band_rows * width
    nblocks = band_rows * per_row
    extended = with_halo(frames_x, (("row", 1),), 1)[0]
    padded = jnp.pad(extended, ((0, 0), (1, 1), (0, 0)))
    total = jnp.zeros((tokens, chans), jnp.float32)
    for row_off in range(3):
        for col_off in range(3):
            window = padded[row_off : row_off + band_rows, col_off : col_off + width].reshape(
                tokens, chans
            )
            total = total + jnp.dot(
                window, conv_weight[row_off, col_off], preferred_element_type=jnp.float32
            )
    feats = (total + conv_bias).astype(jnp.bfloat16)
    queries = normed(feats, query_weight, query_gain)
    keys_own = normed(feats, key_weight, key_gain)
    values_own = jnp.dot(feats, value_weight, preferred_element_type=jnp.float32).astype(
        jnp.bfloat16
    )
    paired = jnp.concatenate([keys_own, values_own], axis=-1).reshape(
        1, band_rows, width, 2 * chans
    )
    earlier = shifted(paired, "frame", 1)
    reached = with_halo(earlier, (("row", 1),), DISP)[0]
    frame_pos = lax.axis_index("frame")
    band_pos = lax.axis_index("row")
    local_ids = source_ids[0] - (band_pos * band_rows - DISP) * per_row
    picked = jnp.take(reached, local_ids, axis=0)
    key_set = jnp.concatenate(
        [keys_own.reshape(nblocks, 1, BLOCK, chans), picked[..., :chans]], axis=1
    )
    value_set = jnp.concatenate(
        [values_own.reshape(nblocks, 1, BLOCK, chans), picked[..., chans:]], axis=1
    )
    key_heads = key_set.reshape(nblocks, -1, HEADS, HD)
    value_heads = value_set.reshape(nblocks, -1, HEADS, HD)
    query_heads = queries.reshape(nblocks, BLOCK, HEADS, HD)
    slots = (jnp.arange(KSRC, dtype=jnp.int32)[None, :] < valid_counts[0][:, None]) & (
        frame_pos > 0
    )
    slot_mask = jnp.concatenate([jnp.ones((nblocks, 1), dtype=bool), slots], axis=1)
    mask = jnp.repeat(slot_mask, BLOCK, axis=1)
    scores = jnp.einsum(
        "nqhd,nkhd->nhqk", query_heads, key_heads, preferred_element_type=jnp.float32
    ) * HD ** (-0.5)
    expo = jnp.where(mask[:, None, None, :], jnp.exp(scores), 0.0)
    probs = (expo / jnp.sum(expo, axis=-1, keepdims=True)).astype(jnp.bfloat16)
    mixed = jnp.einsum("nhqk,nkhd->nqhd", probs, value_heads, preferred_element_type=jnp.float32)
    mixed = mixed.reshape(tokens, chans).astype(jnp.bfloat16)
    result = feats.astype(jnp.float32) + jnp.dot(
        mixed, out_weight, preferred_element_type=jnp.float32
    )
    return result.astype(jnp.bfloat16).reshape(1, band_rows, width, chans)


def solution(mesh):
    return jax.shard_map(
        shards,
        mesh=mesh,
        in_specs=(
            P("frame", "row", None, None),
            P(),
            P(),
            P(),
            P(),
            P(),
            P(),
            P(),
            P(),
            P("frame", "row", None),
            P("frame", "row"),
        ),
        out_specs=P("frame", "row", None, None),
        check_vma=False,
    )
```

profile of v0, /device:TPU:57, one launch (start us, length us, event | category | flops | bytes accessed | tf_op | source)
XLA Modules:
  0.0 182.8 jit_solution(3346453119438340838)
XLA Ops:
  0.0 1.1 fusion.41
  1.1 3.7 %collective-permute-start = (bf16[1,1,128,512]{3,2,1,0:T(8,128)(2,1)S(1)}, bf16[1,1,128,512]{3,2,1,0:T(8,128)(2,1)S(1)}, u32[]{:S(2)}, u32[]{:S(2)}) collective-permute-start(bf16[1,1,128,512]{3,2,1,0:T(8,128)(2,1)S(1)} %get-tuple-element.17), channel_id=1, source_target_pairs={{0,1},{1,2},{2,3},{3,4},{4,5},{5,6},{6,7},{7,8},{8,9},{9,10},{10,1... | collective-permute-start | bytes 393224 | tf_op jit(solution)/shard_map/ppermute | solution.py:20
  4.8 1.9 %collective-permute-start.1 = (bf16[1,1,128,512]{3,2,1,0:T(8,128)(2,1)S(1)}, bf16[1,1,128,512]{3,2,1,0:T(8,128)(2,1)S(1)}, u32[]{:S(2)}, u32[]{:S(2)}) collective-permute-start(bf16[1,1,128,512]{3,2,1,0:T(8,128)(2,1)S(1)} %get-tuple-element.18), channel_id=1, source_target_pairs={{1,0},{2,1},{3,2},{4,3},{5,4},{6,5},{7,6},{8,7},{9,8},{10,9},{11,1... | collective-permute-start | bytes 393224 | tf_op jit(solution)/shard_map/ppermute | solution.py:21
  6.7 2.0 %fusion.17 = f32[768,512]{1,0:T(8,128)S(1)} fusion(bf16[768,512]{1,0:T(8,128)(2,1)} %bitcast.105, bf16[3,3,512,512]{3,2,1,0:T(8,128)(2,1)} %param.12), kind=kOutput, calls=%fused_computation.41 | convolution fusion | flops 402653184 | bytes 2883584 | tf_op jit(solution)/shard_map/dot_general | solution.py:69
  8.7 2.3 %collective-permute-done.1 = bf16[1,1,128,512]{3,2,1,0:T(8,128)(2,1)S(1)} collective-permute-done((bf16[1,1,128,512]{3,2,1,0:T(8,128)(2,1)S(1)}, bf16[1,1,128,512]{3,2,1,0:T(8,128)(2,1)S(1)}, u32[]{:S(2)}, u32[]{:S(2)}) %collective-permute-start.1) | collective-permute-done | bytes 131104 | tf_op jit(solution)/shard_map/ppermute | solution.py:21
  11.1 0.1 pad_maximum_fusion.3
  11.2 0.6 fusion.23
  11.9 0.7 pad_slice_fusion.5
  12.6 0.6 fusion.21
  13.2 0.6 fusion.25
  13.7 0.6 fusion.19
  14.3 0.6 fusion.15
  14.9 0.6 fusion.13
  15.5 0.6 fusion.10
  16.1 1.2 add_convert_fusion.1
  17.3 1.5 convolution_convert_fusion
  18.7 0.6 bitcast_reduce_fusion.1
  19.4 1.3 mul.64
  20.7 3.1 %copy.30 = f32[768,512]{1,0:T(8,128)} copy(f32[768,512]{0,1:T(8,128)} %bitcast.107) | data formatting | bytes 3145728 | tf_op jit(solution)/shard_map/mul | solution.py:35
  23.7 1.6 copy.29
  25.4 2.4 %multiply_convert_fusion = bf16[768,512]{1,0:T(8,128)(2,1)S(1)} fusion(f32[768,512]{1,0:T(8,128)} %copy.29, f32[768,512]{1,0:T(8,128)} %copy.30, f32[512]{0:T(512)S(1)} %copy-done.15), kind=kLoop, calls=%fused_computation.16 | loop fusion | flops 1179648 | bytes 3934208 | tf_op jit(solution)/shard_map/convert_element_type | solution.py:39
  27.7 0.9 copy-done.3
  28.6 1.4 pad_maximum_fusion.2
  30.0 5.0 %collective-permute-start.2 = (bf16[1,6,128,1024]{3,2,1,0:T(8,128)(2,1)}, bf16[1,6,128,1024]{3,2,1,0:T(8,128)(2,1)S(1)}, u32[]{:S(2)}, u32[]{:S(2)}) collective-permute-start(bf16[1,6,128,1024]{3,2,1,0:T(8,128)(2,1)} %bitcast.24), channel_id=1, source_target_pairs={{0,16},{16,32},{32,48},{48,64},{64,80},{80,96},{96,112},{112,128},... | collective-permute-start | bytes 4718600 | tf_op jit(solution)/shard_map/ppermute | solution.py:29
  35.4 68.3 %collective-permute-done.2 = bf16[1,6,128,1024]{3,2,1,0:T(8,128)(2,1)S(1)} collective-permute-done((bf16[1,6,128,1024]{3,2,1,0:T(8,128)(2,1)}, bf16[1,6,128,1024]{3,2,1,0:T(8,128)(2,1)S(1)}, u32[]{:S(2)}, u32[]{:S(2)}) %collective-permute-start.2) | collective-permute-done | bytes 1572896 | tf_op jit(solution)/shard_map/ppermute | solution.py:29
  103.7 1.1 fusion.40
  104.8 4.4 %collective-permute-start.3 = (bf16[1,2,128,1024]{3,2,1,0:T(8,128)(2,1)}, bf16[1,2,128,1024]{3,2,1,0:T(8,128)(2,1)S(1)}, u32[]{:S(2)}, u32[]{:S(2)}) collective-permute-start(bf16[1,2,128,1024]{3,2,1,0:T(8,128)(2,1)} %get-tuple-element.7), channel_id=1, source_target_pairs={{0,1},{1,2},{2,3},{3,4},{4,5},{5,6},{6,7},{7,8},{8,9},{9,10},{10,1... | collective-permute-start | bytes 1572872 | tf_op jit(solution)/shard_map/ppermute | solution.py:20
  109.3 2.1 %collective-permute-start.4 = (bf16[1,2,128,1024]{3,2,1,0:T(8,128)(2,1)}, bf16[1,2,128,1024]{3,2,1,0:T(8,128)(2,1)}, u32[]{:S(2)}, u32[]{:S(2)}) collective-permute-start(bf16[1,2,128,1024]{3,2,1,0:T(8,128)(2,1)} %get-tuple-element.8), channel_id=1, source_target_pairs={{1,0},{2,1},{3,2},{4,3},{5,4},{6,5},{7,6},{8,7},{9,8},{10,9},{11,1... | collective-permute-start | bytes 1572872 | tf_op jit(solution)/shard_map/ppermute | solution.py:21
  111.5 0.6 bitcast_reduce_fusion
  112.2 0.2 fusion.3
  112.4 1.9 %reshape.131 = bf16[6,128,8,64]{1,0,3,2:T(8,128)(2,1)} reshape(bf16[768,512]{0,1:T(8,128)(2,1)S(1)} %fusion.3) | data formatting | bytes 1572864 | tf_op jit(solution)/shard_map/reshape | solution.py:95
  114.3 1.4 collective-permute-done.3
  115.7 4.4 %collective-permute-done.4 = bf16[1,2,128,1024]{3,2,1,0:T(8,128)(2,1)} collective-permute-done((bf16[1,2,128,1024]{3,2,1,0:T(8,128)(2,1)}, bf16[1,2,128,1024]{3,2,1,0:T(8,128)(2,1)}, u32[]{:S(2)}, u32[]{:S(2)}) %collective-permute-start.4) | collective-permute-done | bytes 524320 | tf_op jit(solution)/shard_map/ppermute | solution.py:21
  120.1 1.9 %maximum_bitcast_fusion = bf16[10,128,1024]{2,1,0:T(8,128)(2,1)S(1)} fusion(bf16[1,2,128,1024]{3,2,1,0:T(8,128)(2,1)} %collective-permute-done.4, bf16[1,6,128,1024]{3,2,1,0:T(8,128)(2,1)} %copy-done.8, bf16[1,2,128,1024]{3,2,1,0:T(8,128)(2,1)S(1)} %collective-permute-done.3), kind=kLoop, calls=%fused_computation.8 | loop fusion | flops 2621440 | bytes 5242880 | tf_op jit(solution)/shard_map/squeeze | solution.py:82
  122.0 4.4 %gather_fusion = bf16[24,128,1024]{2,1,0:T(8,128)(2,1)} fusion(bf16[10,128,1024]{2,1,0:T(8,128)(2,1)S(1)} %maximum_bitcast_fusion, s32[1024]{0:T(1024)S(1)} %pad_clamp_fusion), kind=kCustom, calls=%fused_computation | custom fusion | bytes 12583008 | tf_op jit(solution)/shard_map/jit(_take)/gather | solution.py:86
  126.4 3.4 %broadcast_select_fusion = bf16[6,4,128,1024]{3,2,1,0:T(8,128)(2,1)S(1)} fusion(bf16[6,4,128,1024]{3,2,1,0:T(8,128)(2,1)} %bitcast.104, pred[6,4]{1,0:T(8,128)(4,1)S(1)} %copy.28), kind=kLoop, calls=%fused_computation.5 | loop fusion | flops 3145728 | bytes 12582936 | tf_op jit(solution)/shard_map/jit(_take)/select_n | solution.py:86
  129.9 0.9 fusion.39
  130.8 0.2 copy-done.4
  131.0 0.2 copy-done.11
  131.2 3.4 %pad_maximum_fusion = (bf16[6,5,128,512]{3,2,1,0:T(8,128)(2,1)}, bf16[6,5,128,512]{3,2,1,0:T(8,128)(2,1)}) fusion(bf16[6,4,128,512]{3,2,1,0:T(8,128)(2,1)S(1)} %get-tuple-element.6, bf16[6,1,128,512]{3,2,1,0:T(8,128)(2,1)S(1)} %bitcast.115, bf16[6,4,128,512]{3,2,1,0:T(8,128)(2,1)S(1)} %get-tuple-element.5, bf16[6,1,128,512]{3,2,1,0:T(8,128)(2,1)S(1)} %bitcast.106), kind=kLoop, calls=%fused_computation.6 | loop fusion | flops 3932160 | bytes 15728640 | tf_op jit(solution)/shard_map/concatenate | solution.py:90
  134.7 8.1 %copy.33 = bf16[6,5,128,512]{2,1,3,0:T(8,128)(2,1)} copy(bf16[6,5,128,512]{3,2,1,0:T(8,128)(2,1)} %get-tuple-element.25) | data formatting | bytes 7864320 | tf_op jit(solution)/shard_map/concatenate | solution.py:90
  142.8 9.8 %reshape.130 = bf16[6,640,8,64]{1,3,2,0:T(8,128)(2,1)} reshape(bf16[6,5,128,512]{2,1,3,0:T(8,128)(2,1)} %copy.33) | data formatting | bytes 7864320 | tf_op jit(solution)/shard_map/reshape | solution.py:94
  152.5 8.1 %copy.35 = bf16[6,5,128,512]{2,1,3,0:T(8,128)(2,1)} copy(bf16[6,5,128,512]{3,2,1,0:T(8,128)(2,1)} %get-tuple-element.26) | data formatting | bytes 7864320 | tf_op jit(solution)/shard_map/concatenate | solution.py:87
  160.6 9.9 %reshape.133 = bf16[6,640,8,64]{1,3,2,0:T(8,128)(2,1)} reshape(bf16[6,5,128,512]{2,1,3,0:T(8,128)(2,1)} %copy.35) | data formatting | bytes 7864320 | tf_op jit(solution)/shard_map/reshape | solution.py:93
  170.5 5.6 %fusion = (f32[6,8,128]{2,1,0:T(8,128)S(1)}, f32[6,8,128,640]{3,2,1,0:T(8,128)S(1)}) fusion(pred[6,640]{1,0:T(8,128)(4,1)S(1)} %broadcast_bitcast_fusion, bf16[6,640,8,64]{1,3,2,0:T(8,128)(2,1)} %reshape.133, bf16[6,128,8,64]{1,0,3,2:T(8,128)(2,1)S(1)} %copy-done.12), kind=kOutput, calls=%fused_computation.3 | convolution fusion | flops 515106816 | bytes 20475648 | tf_op jit(solution)/shard_map/nqhd,nkhd->nhqk/dot_general | solution.py:101
  176.1 4.6 %fusion.5 = bf16[6,128,8,64]{1,3,2,0:T(8,128)(2,1)S(1)} fusion(bf16[6,640,8,64]{1,3,2,0:T(8,128)(2,1)S(1)} %copy-done.9, f32[6,8,128,640]{3,2,1,0:T(8,128)S(1)} %get-tuple-element.24, f32[6,8,128]{2,1,0:T(8,128)S(1)} %get-tuple-element.23, pred[6,640]{1,0:T(8,128)(4,1)S(1)} %broadcast_bitcast_fusion), kind=kOutput, calls=%fused_computation.20 | convolution fusion | flops 519438336 | bytes 20475648 | tf_op jit(solution)/shard_map/nhqk,nkhd->nqhd/dot_general | solution.py:106
  180.7 0.6 copy.37
  181.3 1.5 add_convert_fusion
  (52 shorter events, 0.6 us)
Async XLA Ops:
  0.0 18.7 %copy-start = (bf16[512,512]{1,0:T(8,128)(2,1)S(1)}, bf16[512,512]{1,0:T(8,128)(2,1)}, u32[]{:S(2)}) copy-start(bf16[512,512]{1,0:T(8,128)(2,1)} %param.15) | copy-start | bytes 1572868
  0.0 11.1 %copy-start.2 = (bf16[1,6,128,512]{3,2,1,0:T(8,128)(2,1)S(1)}, bf16[1,6,128,512]{3,2,1,0:T(8,128)(2,1)}, u32[]{:S(2)}) copy-start(bf16[1,6,128,512]{3,2,1,0:T(8,128)(2,1)} %param.11) | copy-start | bytes 2359300
  1.1 7.6 %collective-permute-start = (bf16[1,1,128,512]{3,2,1,0:T(8,128)(2,1)S(1)}, bf16[1,1,128,512]{3,2,1,0:T(8,128)(2,1)S(1)}, u32[]{:S(2)}, u32[]{:S(2)}) collective-permute-start(bf16[1,1,128,512]{3,2,1,0:T(8,128)(2,1)S(1)} %get-tuple-element.17), channel_id=1, source_target_pairs={{0,1},{1,2},{2,3},{3,4},{4,5},{5,6},{6,7},{7,8},{8,9},{9,10},{10,1... | collective-permute-start | bytes 393224 | tf_op jit(solution)/shard_map/ppermute | solution.py:20
  4.8 6.3 %collective-permute-start.1 = (bf16[1,1,128,512]{3,2,1,0:T(8,128)(2,1)S(1)}, bf16[1,1,128,512]{3,2,1,0:T(8,128)(2,1)S(1)}, u32[]{:S(2)}, u32[]{:S(2)}) collective-permute-start(bf16[1,1,128,512]{3,2,1,0:T(8,128)(2,1)S(1)} %get-tuple-element.18), channel_id=1, source_target_pairs={{1,0},{2,1},{3,2},{4,3},{5,4},{6,5},{7,6},{8,7},{9,8},{10,9},{11,1... | collective-permute-start | bytes 393224 | tf_op jit(solution)/shard_map/ppermute | solution.py:21
  6.7 4.5 %copy-start.7 = (bf16[3,3,512,512]{3,2,1,0:T(8,128)(2,1)S(1)}, bf16[3,3,512,512]{3,2,1,0:T(8,128)(2,1)}, u32[]{:S(2)}) copy-start(bf16[3,3,512,512]{3,2,1,0:T(8,128)(2,1)} %param.12) | copy-start | bytes 14155780
  14.9 1.1 copy-start.17
  16.0 1.2 copy-start.18
  17.3 94.2 %copy-start.5 = (bf16[768,512]{1,0:T(8,128)(2,1)}, bf16[768,512]{1,0:T(8,128)(2,1)S(1)}, u32[]{:S(2)}) copy-start(bf16[768,512]{1,0:T(8,128)(2,1)S(1)} %add_convert_fusion.1) | copy-start | bytes 2359300
  20.7 4.7 %copy-start.15 = (f32[512]{0:T(512)S(1)}, f32[512]{0:T(512)}, u32[]{:S(2)}) copy-start(f32[512]{0:T(512)} %param.19) | copy-start | bytes 6148
  25.3 3.3 %copy-start.10 = (bf16[768,512]{1,0:T(8,128)(2,1)S(1)}, bf16[768,512]{1,0:T(8,128)(2,1)}, u32[]{:S(2)}) copy-start(bf16[768,512]{1,0:T(8,128)(2,1)} %convolution_convert_fusion) | copy-start | bytes 2359300
  25.3 9.7 %copy-start.14 = (s32[1,6,4]{1,2,0:T(4,128)S(1)}, s32[1,6,4]{1,2,0:T(4,128)}, u32[]{:S(2)}) copy-start(s32[1,6,4]{1,2,0:T(4,128)} %param.20) | copy-start | bytes 292
  25.4 9.9 %copy-start.20 = (s32[1,6]{1,0:T(1,128)S(1)}, s32[1,6]{1,0:T(1,128)}, u32[]{:S(2)}) copy-start(s32[1,6]{1,0:T(1,128)} %param.21) | copy-start | bytes 76
  27.7 0.9 copy-start.3
  28.6 82.9 %copy-start.13 = (bf16[512,512]{1,0:T(8,128)(2,1)S(1)}, bf16[512,512]{1,0:T(8,128)(2,1)}, u32[]{:S(2)}) copy-start(bf16[512,512]{1,0:T(8,128)(2,1)} %param.14) | copy-start | bytes 1572868
  30.0 82.1 %copy-start.16 = (f32[512]{0:T(512)S(1)}, f32[512]{0:T(512)}, u32[]{:S(2)}) copy-start(f32[512]{0:T(512)} %param.18) | copy-start | bytes 6148
  30.0 73.7 %collective-permute-start.2 = (bf16[1,6,128,1024]{3,2,1,0:T(8,128)(2,1)}, bf16[1,6,128,1024]{3,2,1,0:T(8,128)(2,1)S(1)}, u32[]{:S(2)}, u32[]{:S(2)}) collective-permute-start(bf16[1,6,128,1024]{3,2,1,0:T(8,128)(2,1)} %bitcast.24), channel_id=1, source_target_pairs={{0,16},{16,32},{32,48},{48,64},{64,80},{80,96},{96,112},{112,128},... | collective-permute-start | bytes 4718600 | tf_op jit(solution)/shard_map/ppermute | solution.py:29
  103.7 8.7 %copy-start.8 = (bf16[1,6,128,1024]{3,2,1,0:T(8,128)(2,1)}, bf16[1,6,128,1024]{3,2,1,0:T(8,128)(2,1)S(1)}, u32[]{:S(2)}) copy-start(bf16[1,6,128,1024]{3,2,1,0:T(8,128)(2,1)S(1)} %collective-permute-done.2) | copy-start | bytes 4718596
  104.8 10.8 %collective-permute-start.3 = (bf16[1,2,128,1024]{3,2,1,0:T(8,128)(2,1)}, bf16[1,2,128,1024]{3,2,1,0:T(8,128)(2,1)S(1)}, u32[]{:S(2)}, u32[]{:S(2)}) collective-permute-start(bf16[1,2,128,1024]{3,2,1,0:T(8,128)(2,1)} %get-tuple-element.7), channel_id=1, source_target_pairs={{0,1},{1,2},{2,3},{3,4},{4,5},{5,6},{6,7},{7,8},{8,9},{9,10},{10,1... | collective-permute-start | bytes 1572872 | tf_op jit(solution)/shard_map/ppermute | solution.py:20
  109.3 10.8 %collective-permute-start.4 = (bf16[1,2,128,1024]{3,2,1,0:T(8,128)(2,1)}, bf16[1,2,128,1024]{3,2,1,0:T(8,128)(2,1)}, u32[]{:S(2)}, u32[]{:S(2)}) collective-permute-start(bf16[1,2,128,1024]{3,2,1,0:T(8,128)(2,1)} %get-tuple-element.8), channel_id=1, source_target_pairs={{1,0},{2,1},{3,2},{4,3},{5,4},{6,5},{7,6},{8,7},{9,8},{10,9},{11,1... | collective-permute-start | bytes 1572872 | tf_op jit(solution)/shard_map/ppermute | solution.py:21
  129.9 1.1 copy-start.4
  129.9 1.4 copy-start.11
  160.6 9.9 %copy-start.12 = (bf16[6,128,8,64]{1,0,3,2:T(8,128)(2,1)S(1)}, bf16[6,128,8,64]{1,0,3,2:T(8,128)(2,1)}, u32[]{:S(2)}) copy-start(bf16[6,128,8,64]{1,0,3,2:T(8,128)(2,1)} %reshape.131) | copy-start | bytes 2359300
  170.5 5.6 %copy-start.9 = (bf16[6,640,8,64]{1,3,2,0:T(8,128)(2,1)S(1)}, bf16[6,640,8,64]{1,3,2,0:T(8,128)(2,1)}, u32[]{:S(2)}) copy-start(bf16[6,640,8,64]{1,3,2,0:T(8,128)(2,1)} %reshape.130) | copy-start | bytes 11796484
  176.1 5.2 %copy-start.6 = (bf16[768,512]{1,0:T(8,128)(2,1)S(1)}, bf16[768,512]{1,0:T(8,128)(2,1)}, u32[]{:S(2)}) copy-start(bf16[768,512]{1,0:T(8,128)(2,1)} %copy-done.5) | copy-start | bytes 2359300
  176.1 5.2 %copy-start.19 = (bf16[512,512]{1,0:T(8,128)(2,1)S(1)}, bf16[512,512]{1,0:T(8,128)(2,1)}, u32[]{:S(2)}) copy-start(bf16[512,512]{1,0:T(8,128)(2,1)} %param.17) | copy-start | bytes 1572868
  176.1 6.7 %copy-start.1 = (bf16[512,512]{1,0:T(8,128)(2,1)S(1)}, bf16[512,512]{1,0:T(8,128)(2,1)}, u32[]{:S(2)}) copy-start(bf16[512,512]{1,0:T(8,128)(2,1)} %param.15) | copy-start | bytes 1572868
where the time goes:
time: 186 us; the launch traced here: 183 us
  waiting for transfers between devices  76.5 us (41%)
  local copies, waits for them, and re-layouts  54.2 us (29%)
  matrix products  21.5 us (12%)
  starting transfers between devices  17.1 us (9%)
  other arithmetic  13.1 us (7%)
    ppermute x1, waiting for transfers between devices, shifted(): return lax.ppermute(block, axis, route)  68.3 us
    reshape x1, local copies, waits for them, and re-layouts, shards(): key_heads = key_set.reshape(nblocks, -1, HEADS, HD)  9.87 us
    reshape x1, local copies, waits for them, and re-layouts, shards(): value_heads = value_set.reshape(nblocks, -1, HEADS, HD)  9.76 us
    concatenate x1, local copies, waits for them, and re-layouts, shards(): jnp.concatenate([values_own.reshape(nblocks, 1, BLOCK, chans), picked[......  8.1 us
    concatenate x1, local copies, waits for them, and re-layouts, shards(): jnp.concatenate([keys_own.reshape(nblocks, 1, BLOCK, chans), picked[...,...  8.1 us
    ppermute x2, starting transfers between devices, with_halo(): before = lax.ppermute(last, axis, up)  8.1 us
    dot_general x9, matrix products, shards(): jnp.dot(window, conv_weight[row_off, col_off], preferred_element_type=jnp...  7.14 us
    ppermute x2, waiting for transfers between devices, with_halo(): after = lax.ppermute(initial, axis, down)  6.74 us
  transfers between devices with their start and end apart: 5, of which 4 were waited for; matrix products, arithmetic and copies ran while one was open for 3% of the time, Pallas kernels for 0%

commit v1 on v0

v1 whole, which is shorter than its diff:
```python
import functools

import jax
import jax.numpy as jnp
from jax import lax
from jax.experimental import pallas as pl
from jax.experimental.pallas import tpu as pltpu
from jax.sharding import PartitionSpec as P

HEADS = 8
HD = 64
KSRC = 4
BLOCK = 128
DISP = 2
PAIR = 2 * HD
VMEM_BYTES = 48 * 1024 * 1024

NT = (((1,), (1,)), ((), ()))


def dot(a, b):
    return jnp.dot(a, b, preferred_element_type=jnp.float32)


def shifted_sum(y_left, y_mid, y_right):
    tokens = y_mid.shape[0]
    column = lax.broadcasted_iota(jnp.int32, y_mid.shape, 0) % BLOCK
    left = jnp.where(column == 0, 0.0, pltpu.roll(y_left, 1, 0))
    right = jnp.where(column == BLOCK - 1, 0.0, pltpu.roll(y_right, tokens - 1, 0))
    return left + y_mid + right


def conv_inner_kernel(x_ref, w_ref, b_ref, out_ref, acc_ref):
    tokens = out_ref.shape[0]
    step = pl.program_id(0)
    y = sum(dot(x_ref[pl.ds(a * BLOCK, tokens)], w_ref[a, 0]) for a in range(3))
    column = lax.broadcasted_iota(jnp.int32, y.shape, 0) % BLOCK

    @pl.when(step == 0)
    def _():
        acc_ref[...] = jnp.where(column == 0, 0.0, pltpu.roll(y, 1, 0)) + b_ref[...]

    @pl.when(step == 1)
    def _():
        acc_ref[...] += y

    @pl.when(step == 2)
    def _():
        right = jnp.where(column == BLOCK - 1, 0.0, pltpu.roll(y, tokens - 1, 0))
        out_ref[...] = (acc_ref[...] + right).astype(jnp.bfloat16)


def conv_edge_kernel(before_ref, top_ref, bottom_ref, after_ref, w_ref, b_ref, out_ref, acc_ref):
    tokens = out_ref.shape[0]
    step = pl.program_id(0)
    upper = [before_ref[...], top_ref[pl.ds(0, BLOCK)], top_ref[pl.ds(BLOCK, BLOCK)]]
    lower = [bottom_ref[pl.ds(0, BLOCK)], bottom_ref[pl.ds(BLOCK, BLOCK)], after_ref[...]]
    y = sum(dot(jnp.concatenate([upper[a], lower[a]], 0), w_ref[a, 0]) for a in range(3))
    column = lax.broadcasted_iota(jnp.int32, y.shape, 0) % BLOCK

    @pl.when(step == 0)
    def _():
        acc_ref[...] = jnp.where(column == 0, 0.0, pltpu.roll(y, 1, 0)) + b_ref[...]

    @pl.when(step == 1)
    def _():
        acc_ref[...] += y

    @pl.when(step == 2)
    def _():
        right = jnp.where(column == BLOCK - 1, 0.0, pltpu.roll(y, tokens - 1, 0))
        out_ref[...] = (acc_ref[...] + right).astype(jnp.bfloat16)


def head_norm(proj, gain):
    squares = (proj * proj).astype(jnp.bfloat16)
    row = lax.broadcasted_iota(jnp.int32, (4 * HD, 4 * HD), 0) // HD
    col = lax.broadcasted_iota(jnp.int32, (4 * HD, 4 * HD), 1) // HD
    mean_of = jnp.where(row == col, 1.0 / HD, 0.0).astype(jnp.bfloat16)
    wide = 4 * HD
    means = [dot(squares[:, i : i + wide], mean_of) for i in range(0, HEADS * HD, wide)]
    mean = jnp.concatenate(means, 1)
    return (proj * lax.rsqrt(mean + 1e-06) * gain).astype(jnp.bfloat16)


def pair_product(q, k, v):
    low = lax.broadcasted_iota(jnp.int32, (BLOCK, PAIR), 1) < HD
    zero = jnp.zeros((BLOCK, PAIR), jnp.bfloat16)
    one = jnp.ones((BLOCK, PAIR), jnp.bfloat16)
    keys = jnp.concatenate([jnp.where(low, k, zero), jnp.where(low, zero, k)], 0)
    scores = lax.dot_general(q, keys, NT, preferred_element_type=jnp.float32)
    expo = jnp.exp(scores).astype(jnp.bfloat16)
    upper = jnp.concatenate([jnp.where(low, v, zero), jnp.where(low, one, zero)], 1)
    lower = jnp.concatenate([jnp.where(low, zero, v), jnp.where(low, zero, one)], 1)
    return dot(expo, jnp.concatenate([upper, lower], 0))


def own_kernel(f_ref, wq_ref, wk_ref, wv_ref, gq_ref, gk_ref, q_ref, sums_ref, norms_ref, k_ref, v_ref):
    feats = f_ref[...]
    q_ref[...] = head_norm(dot(feats, wq_ref[...]), gq_ref[...] * HD**-0.5)
    k_ref[...] = head_norm(dot(feats, wk_ref[...]), gk_ref[...])
    v_ref[...] = dot(feats, wv_ref[...]).astype(jnp.bfloat16)

    @pl.loop(0, f_ref.shape[0] // BLOCK)
    def _(block):
        rows = pl.ds(pl.multiple_of(block * BLOCK, BLOCK), BLOCK)
        for p in range(HEADS // 2):
            cols = pl.ds(p * PAIR, PAIR)
            both = pair_product(q_ref[rows, cols], k_ref[rows, cols], v_ref[rows, cols])
            sums_ref[rows, cols] = both[:, :PAIR]
            norms_ref[rows, cols] = both[:, PAIR:]


def last_kernel(
    ids_ref, counts_ref, up_ref, prev_ref, down_ref, f_ref, q_ref, sums_in_ref, norms_in_ref,
    wk_ref, wv_ref, wo_ref, gk_ref, out_ref, k_ref, v_ref, sums_ref, norms_ref,
):
    halo = DISP * BLOCK
    inner = prev_ref.shape[0]
    for ref, start in ((up_ref, 0), (prev_ref, halo), (down_ref, halo + inner)):
        feats = ref[...]
        rows = pl.ds(start, feats.shape[0])
        k_ref[rows] = head_norm(dot(feats, wk_ref[...]), gk_ref[...])
        v_ref[rows] = dot(feats, wv_ref[...]).astype(jnp.bfloat16)
    sums_ref[...] = sums_in_ref[...]
    norms_ref[...] = norms_in_ref[...]
    for block in range(f_ref.shape[0] // BLOCK):
        rows = pl.ds(block * BLOCK, BLOCK)

        @pl.loop(0, counts_ref[block])
        def _(slot):
            src = pl.ds(pl.multiple_of(ids_ref[block, slot] * BLOCK, BLOCK), BLOCK)
            for p in range(HEADS // 2):
                cols = pl.ds(p * PAIR, PAIR)
                both = pair_product(q_ref[rows, cols], k_ref[src, cols], v_ref[src, cols])
                sums_ref[rows, cols] += both[:, :PAIR]
                norms_ref[rows, cols] += both[:, PAIR:]

    mixed = (sums_ref[...] / norms_ref[...]).astype(jnp.bfloat16)
    result = f_ref[...].astype(jnp.float32) + dot(mixed, wo_ref[...])
    out_ref[...] = result.astype(jnp.bfloat16)


def params(**kw):
    return pltpu.CompilerParams(vmem_limit_bytes=VMEM_BYTES, **kw)


def cost(flops, moved):
    return pl.CostEstimate(flops=int(flops), bytes_accessed=int(moved), transcendentals=0)


def conv_inner(x, weight, bias):
    tokens, chans = x.shape[0] - 2 * BLOCK, x.shape[1]
    return pl.pallas_call(
        conv_inner_kernel,
        grid=(3,),
        in_specs=[
            pl.BlockSpec(x.shape, lambda i: (0, 0)),
            pl.BlockSpec((3, 1, chans, chans), lambda i: (0, i, 0, 0)),
            pl.BlockSpec((1, chans), lambda i: (0, 0)),
        ],
        out_specs=pl.BlockSpec((tokens, chans), lambda i: (0, 0)),
        out_shape=jax.ShapeDtypeStruct((tokens, chans), jnp.bfloat16),
        scratch_shapes=[pltpu.VMEM((tokens, chans), jnp.float32)],
        compiler_params=params(),
        cost_estimate=cost(18 * tokens * chans * chans, 2 * weight.size + 4 * x.size),
        name="conv_inner",
    )(x, weight, bias)


def conv_edge(before, x, after, weight, bias):
    tokens, chans = 2 * BLOCK, x.shape[1]
    last = x.shape[0] // tokens - 1
    return pl.pallas_call(
        conv_edge_kernel,
        grid=(3,),
        in_specs=[
            pl.BlockSpec((BLOCK, chans), lambda i: (0, 0)),
            pl.BlockSpec((tokens, chans), lambda i: (0, 0)),
            pl.BlockSpec((tokens, chans), lambda i: (last, 0)),
            pl.BlockSpec((BLOCK, chans), lambda i: (0, 0)),
            pl.BlockSpec((3, 1, chans, chans), lambda i: (0, i, 0, 0)),
            pl.BlockSpec((1, chans), lambda i: (0, 0)),
        ],
        out_specs=pl.BlockSpec((tokens, chans), lambda i: (0, 0)),
        out_shape=jax.ShapeDtypeStruct((tokens, chans), jnp.bfloat16),
        scratch_shapes=[pltpu.VMEM((tokens, chans), jnp.float32)],
        compiler_params=params(),
        cost_estimate=cost(18 * tokens * chans * chans, 2 * weight.size + 4 * x.size),
        name="conv_edge",
    )(before, x, x, after, weight, bias)


def own_part(feats, wq, wk, wv, gq, gk):
    tokens, chans = feats.shape
    return pl.pallas_call(
        own_kernel,
        out_shape=[
            jax.ShapeDtypeStruct((tokens, chans), jnp.bfloat16),
            jax.ShapeDtypeStruct((tokens, chans), jnp.float32),
            jax.ShapeDtypeStruct((tokens, chans), jnp.float32),
        ],
        scratch_shapes=[pltpu.VMEM((tokens, chans), jnp.bfloat16)] * 2,
        compiler_params=params(),
        cost_estimate=cost(10 * tokens * chans * chans, 12 * feats.size + 6 * wq.size),
        name="own_part",
    )(feats, wq, wk, wv, gq, gk)


def last_part(ids, counts, up, prev, down, feats, q, sums, norms, wk, wv, wo, gk):
    tokens, chans = feats.shape
    reach = up.shape[0] + prev.shape[0] + down.shape[0]
    smem = pl.BlockSpec(memory_space=pltpu.SMEM)
    vmem = pl.BlockSpec(memory_space=pltpu.VMEM)
    return pl.pallas_call(
        last_kernel,
        in_specs=[smem, smem] + [vmem] * 11,
        out_specs=vmem,
        out_shape=jax.ShapeDtypeStruct((tokens, chans), jnp.bfloat16),
        scratch_shapes=[pltpu.VMEM((reach, chans), jnp.bfloat16)] * 2
        + [pltpu.VMEM((tokens, chans), jnp.float32)] * 2,
        compiler_params=params(),
        cost_estimate=cost(16 * tokens * chans * chans, 20 * feats.size + 6 * wk.size),
        name="last_part",
    )(ids, counts, up, prev, down, feats, q, sums, norms, wk, wv, wo, gk)


def passed_on(array, axis, distance):
    devices = range(lax.axis_size(axis))
    return lax.ppermute(array, axis, [(i, i + distance) for i in devices if i + distance in devices])


def shards(
    frames_x, conv_weight, conv_bias, query_weight, key_weight, value_weight, out_weight,
    query_gain, key_gain, source_ids, valid_counts,
):
    _, band_rows, width, chans = frames_x.shape
    tokens = band_rows * width
    halo = DISP * BLOCK
    x = frames_x.reshape(tokens, chans)
    bias = conv_bias.reshape(1, chans)
    gq = query_gain.reshape(1, chans)
    gk = key_gain.reshape(1, chans)
    before = passed_on(x[tokens - BLOCK :], "row", 1)
    after = passed_on(x[:BLOCK], "row", -1)
    inner = conv_inner(x, conv_weight, bias)
    edges = conv_edge(before, x, after, conv_weight, bias)
    feats = jnp.concatenate([edges[:BLOCK], inner, edges[BLOCK:]], 0)
    prev = passed_on(feats, "frame", 1)
    q, sums, norms = own_part(feats, query_weight, key_weight, value_weight, gq, gk)
    up = passed_on(prev[tokens - halo :], "row", 1)
    down = passed_on(prev[:halo], "row", -1)
    frame_pos = lax.axis_index("frame")
    band_pos = lax.axis_index("row")
    ids = jnp.clip(source_ids[0] - (band_pos * band_rows - DISP), 0, band_rows + 2 * DISP - 1)
    counts = jnp.where(frame_pos > 0, valid_counts[0], 0)
    out = last_part(
        ids, counts, up, prev, down, feats, q, sums, norms, key_weight, value_weight, out_weight, gk
    )
    return out.reshape(1, band_rows, width, chans)


def solution(mesh):
    return jax.shard_map(
        shards,
        mesh=mesh,
        in_specs=(
            P("frame", "row", None, None),
            P(), P(), P(), P(), P(), P(), P(), P(),
            P("frame", "row", None),
            P("frame", "row"),
        ),
        out_specs=P("frame", "row", None, None),
        check_vma=False,
    )
```

time: 186 us -> 86.9 us (0.47)
  the two profiles are of different devices: /device:TPU:57 before, /device:TPU:40 now
where the time goes in v1:
time: 86.9 us; the launch traced here: 85.9 us
  waiting for transfers between devices  38.9 us (45%)
  Pallas kernels  23.6 us (27%)
  starting transfers between devices  16.9 us (19%)
  local copies, waits for them, and re-layouts  6.11 us (7%)
    ppermute x5, waiting for transfers between devices, passed_on(): lax.ppermute(array, axis, [(i, i + distance) for i in devices if i + dist...  38.9 us
    ppermute x5, starting transfers between devices, passed_on(): lax.ppermute(array, axis, [(i, i + distance) for i in devices if i + dist...  16.9 us
    pallas_call x1, Pallas kernels, last_part(): pl.pallas_call(last_kernel, in_specs=[smem, smem] + [vmem] * 11, out_spec...  12.2 us
    pallas_call x1, Pallas kernels, own_part(): pl.pallas_call(own_kernel, out_shape=[jax.ShapeDtypeStruct((tokens, chans...  5.5 us
    unnamed x26, local copies, waits for them, and re-layouts  4.2 us
    pallas_call x1, Pallas kernels, conv_inner(): pl.pallas_call(conv_inner_kernel, grid=(3,), in_specs=[pl.BlockSpec(x.sha...  3.63 us
    pallas_call x1, Pallas kernels, conv_edge(): pl.pallas_call(conv_edge_kernel, grid=(3,), in_specs=[pl.BlockSpec((BLOCK...  2.27 us
  transfers between devices with their start and end apart: 5, of which 2 were waited for; matrix products, arithmetic and copies ran while one was open for 0% of the time, Pallas kernels for 11%

profile of v1, /device:TPU:40, one launch (start us, length us, event | category | flops | bytes accessed | tf_op | source)
XLA Modules:
  0.0 85.9 jit_solution(5987982679364788324)
XLA Ops:
  0.0 1.0 %slice_bitcast_fusion = (bf16[128,512]{1,0:T(8,128)(2,1)S(1)}, bf16[128,512]{1,0:T(8,128)(2,1)S(1)}) fusion(bf16[1,6,128,512]{3,2,1,0:T(8,128)(2,1)} %param.11), kind=kLoop, calls=%fused_computation.1 | loop fusion | bytes 524288 | tf_op jit(solution)/shard_map/slice | solution.py:245
  1.0 3.7 %collective-permute-start.1 = (bf16[128,512]{1,0:T(8,128)(2,1)S(1)}, bf16[128,512]{1,0:T(8,128)(2,1)S(1)}, u32[]{:S(2)}, u32[]{:S(2)}) collective-permute-start(bf16[128,512]{1,0:T(8,128)(2,1)S(1)} %get-tuple-element.13), channel_id=1, source_target_pairs={{1,0},{2,1},{3,2},{4,3},{5,4},{6,5},{7,6},{8,7},{9,8},{10,9},{11,1... | collective-permute-start | bytes 393224 | tf_op jit(solution)/shard_map/ppermute | solution.py:230
  4.6 1.9 %collective-permute-start = (bf16[128,512]{1,0:T(8,128)(2,1)S(1)}, bf16[128,512]{1,0:T(8,128)(2,1)S(1)}, u32[]{:S(2)}, u32[]{:S(2)}) collective-permute-start(bf16[128,512]{1,0:T(8,128)(2,1)S(1)} %get-tuple-element.14), channel_id=1, source_target_pairs={{0,1},{1,2},{2,3},{3,4},{4,5},{5,6},{6,7},{7,8},{8,9},{9,10},{10,1... | collective-permute-start | bytes 393224 | tf_op jit(solution)/shard_map/ppermute | solution.py:230
  6.6 0.0 copy-start
  6.6 2.3 %copy-done = bf16[3,3,512,512]{3,2,1,0:T(8,128)(2,1)S(1)} copy-done((bf16[3,3,512,512]{3,2,1,0:T(8,128)(2,1)S(1)}, bf16[3,3,512,512]{3,2,1,0:T(8,128)(2,1)}, u32[]{:S(2)}) %copy-start) | copy-done | bytes 4718616
  8.9 0.0 copy-start.2
  8.9 1.1 %copy-done.2 = bf16[1,6,128,512]{3,2,1,0:T(8,128)(2,1)S(1)} copy-done((bf16[1,6,128,512]{3,2,1,0:T(8,128)(2,1)S(1)}, bf16[1,6,128,512]{3,2,1,0:T(8,128)(2,1)}, u32[]{:S(2)}) %copy-start.2) | copy-done | bytes 786456
  10.1 0.0 copy-start.4
  10.1 0.7 copy-done.4
  10.7 0.0 copy-start.1
  10.7 0.0 copy-start.3
  10.7 3.6 %conv_inner.1 = bf16[512,512]{1,0:T(8,128)(2,1)S(1)} custom-call(bf16[768,512]{1,0:T(8,128)(2,1)S(1)} %bitcast.13, bf16[3,3,512,512]{3,2,1,0:T(8,128)(2,1)S(1)} %copy-done, f32[1,512]{1,0:T(1,128)S(1)} %bitcast.16), custom_call_target="tpu_custom_call" | custom-call | flops 2415919104 | bytes 6291456 | tf_op jit(solution)/shard_map/conv_inner/pallas_call | solution.py:154
  14.4 0.0 collective-permute-done.1.after_ref
  14.4 0.0 collective-permute-done.before_ref
  14.4 0.0 copy-done.1
  14.4 0.0 copy-done.3
  14.4 2.3 %conv_edge.1 = bf16[256,512]{1,0:T(8,128)(2,1)S(1)} custom-call(bf16[128,512]{1,0:T(8,128)(2,1)S(1)} %collective-permute-done.before_ref, bf16[768,512]{1,0:T(8,128)(2,1)S(1)} %bitcast.14, bf16[768,512]{1,0:T(8,128)(2,1)S(1)} %bitcast.15, bf16[128,512]{1,0:T(8,128)(2,1)S(1)} %collective-permute-done.1.after_ref, bf16[3,3,512,512]{3,2,1,0:T(8,128)(2,1)S(1)} %copy-done.1, ...), custom_call_target="tpu_custom_call" | custom-call | flops 1207959552 | bytes 6291456 | tf_op jit(solution)/shard_map/conv_edge/pallas_call | solution.py:174
  16.7 0.0 copy-start.11
  16.7 0.0 copy-start.12
  16.7 0.0 copy-start.5
  16.7 0.0 copy-start.6
  16.7 0.0 copy-start.7
  16.8 0.0 copy-start.9
  16.8 0.0 copy-start.10
  16.8 0.1 pad_maximum_fusion.f_ref
  16.9 5.3 %collective-permute-start.2 = (bf16[768,512]{1,0:T(8,128)(2,1)S(1)}, bf16[768,512]{1,0:T(8,128)(2,1)S(1)}, u32[]{:S(2)}, u32[]{:S(2)}) collective-permute-start(bf16[768,512]{1,0:T(8,128)(2,1)S(1)} %pad_maximum_fusion.f_ref), channel_id=1, source_target_pairs={{0,16},{16,32},{32,48},{48,64},{64,80},{80,96},{96,112},{112,128},... | collective-permute-start | bytes 2359304 | tf_op jit(solution)/shard_map/ppermute | solution.py:230
  22.2 0.0 copy-done.11
  22.2 36.4 %collective-permute-done.2.prev_ref = bf16[768,512]{1,0:T(8,128)(2,1)S(1)} collective-permute-done((bf16[768,512]{1,0:T(8,128)(2,1)S(1)}, bf16[768,512]{1,0:T(8,128)(2,1)S(1)}, u32[]{:S(2)}, u32[]{:S(2)}) %collective-permute-start.2) | collective-permute-done | bytes 786464 | tf_op jit(solution)/shard_map/ppermute | solution.py:230
  58.6 0.8 fusion.1
  59.4 4.1 %collective-permute-start.4 = (bf16[256,512]{1,0:T(8,128)(2,1)}, bf16[256,512]{1,0:T(8,128)(2,1)S(1)}, u32[]{:S(2)}, u32[]{:S(2)}) collective-permute-start(bf16[256,512]{1,0:T(8,128)(2,1)} %get-tuple-element.11), channel_id=1, source_target_pairs={{1,0},{2,1},{3,2},{4,3},{5,4},{6,5},{7,6},{8,7},{9,8},{10,9},{11,1... | collective-permute-start | bytes 786440 | tf_op jit(solution)/shard_map/ppermute | solution.py:230
  63.5 1.9 %collective-permute-start.3 = (bf16[256,512]{1,0:T(8,128)(2,1)}, bf16[256,512]{1,0:T(8,128)(2,1)}, u32[]{:S(2)}, u32[]{:S(2)}) collective-permute-start(bf16[256,512]{1,0:T(8,128)(2,1)} %get-tuple-element.12), channel_id=1, source_target_pairs={{0,1},{1,2},{2,3},{3,4},{4,5},{5,6},{6,7},{7,8},{8,9},{9,10},{10,1... | collective-permute-start | bytes 786440 | tf_op jit(solution)/shard_map/ppermute | solution.py:230
  65.5 0.0 copy-done.12
  65.5 0.1 copy.12.ids_ref
  65.6 0.0 copy-done.5
  65.6 0.0 copy-done.6
  65.6 0.0 copy-done.7
  65.6 0.0 copy-done.9
  65.6 0.0 copy-done.10
  65.6 0.0 copy-start.8
  65.6 5.5 %own_part.1 = (bf16[768,512]{1,0:T(8,128)(2,1)S(1)}, f32[768,512]{1,0:T(8,128)S(1)}, f32[768,512]{1,0:T(8,128)}) custom-call(bf16[768,512]{1,0:T(8,128)(2,1)S(1)} %pad_maximum_fusion.f_ref, bf16[512,512]{1,0:T(8,128)(2,1)S(1)} %copy-done.5, bf16[512,512]{1,0:T(8,128)(2,1)S(1)} %copy-done.6, bf16[512,512]{1,0:T(8,128)(2,1)S(1)} %copy-done.7, ...), custom_call_target="tpu_custom_call" | custom-call | flops 2013265920 | bytes 6291456 | tf_op jit(solution)/shard_map/own_part/pallas_call | solution.py:196
  71.1 0.0 collective-permute-done.4.down_ref
  71.1 2.5 %collective-permute-done.3.up_ref = bf16[256,512]{1,0:T(8,128)(2,1)} collective-permute-done((bf16[256,512]{1,0:T(8,128)(2,1)}, bf16[256,512]{1,0:T(8,128)(2,1)}, u32[]{:S(2)}, u32[]{:S(2)}) %collective-permute-start.3) | collective-permute-done | bytes 262176 | tf_op jit(solution)/shard_map/ppermute | solution.py:230
  73.7 0.0 copy-done.8
  73.7 12.2 %last_part.1 = bf16[768,512]{1,0:T(8,128)(2,1)} custom-call(s32[6,4]{1,0:T(8,128)S(1)} %copy.12.ids_ref, s32[6]{0:T(128)S(1)} %fusion.counts_ref, bf16[256,512]{1,0:T(8,128)(2,1)} %collective-permute-done.3.up_ref, bf16[768,512]{1,0:T(8,128)(2,1)S(1)} %collective-permute-done.2.prev_ref, bf16[256,512]{1,0:T(8,128)(2,1)S(1)} %collective-permute-done.4.down_ref, ...), custom_call_target="tpu_custom_call" | custom-call | flops 3221225472 | bytes 9437184 | tf_op jit(solution)/shard_map/last_part/pallas_call | solution.py:215
  (3 shorter events, 0.0 us)
Async XLA Ops:
  1.0 13.4 %collective-permute-start.1 = (bf16[128,512]{1,0:T(8,128)(2,1)S(1)}, bf16[128,512]{1,0:T(8,128)(2,1)S(1)}, u32[]{:S(2)}, u32[]{:S(2)}) collective-permute-start(bf16[128,512]{1,0:T(8,128)(2,1)S(1)} %get-tuple-element.13), channel_id=1, source_target_pairs={{1,0},{2,1},{3,2},{4,3},{5,4},{6,5},{7,6},{8,7},{9,8},{10,9},{11,1... | collective-permute-start | bytes 393224 | tf_op jit(solution)/shard_map/ppermute | solution.py:230
  4.6 9.7 %collective-permute-start = (bf16[128,512]{1,0:T(8,128)(2,1)S(1)}, bf16[128,512]{1,0:T(8,128)(2,1)S(1)}, u32[]{:S(2)}, u32[]{:S(2)}) collective-permute-start(bf16[128,512]{1,0:T(8,128)(2,1)S(1)} %get-tuple-element.14), channel_id=1, source_target_pairs={{0,1},{1,2},{2,3},{3,4},{4,5},{5,6},{6,7},{7,8},{8,9},{9,10},{10,1... | collective-permute-start | bytes 393224 | tf_op jit(solution)/shard_map/ppermute | solution.py:230
  6.6 2.3 %copy-start = (bf16[3,3,512,512]{3,2,1,0:T(8,128)(2,1)S(1)}, bf16[3,3,512,512]{3,2,1,0:T(8,128)(2,1)}, u32[]{:S(2)}) copy-start(bf16[3,3,512,512]{3,2,1,0:T(8,128)(2,1)} %w_ref.3) | copy-start | bytes 14155780
  8.9 1.1 %copy-start.2 = (bf16[1,6,128,512]{3,2,1,0:T(8,128)(2,1)S(1)}, bf16[1,6,128,512]{3,2,1,0:T(8,128)(2,1)}, u32[]{:S(2)}) copy-start(bf16[1,6,128,512]{3,2,1,0:T(8,128)(2,1)} %param.11) | copy-start | bytes 2359300
  10.1 0.7 copy-start.4
  10.7 3.7 %copy-start.1 = (bf16[3,3,512,512]{3,2,1,0:T(8,128)(2,1)S(1)}, bf16[3,3,512,512]{3,2,1,0:T(8,128)(2,1)}, u32[]{:S(2)}) copy-start(bf16[3,3,512,512]{3,2,1,0:T(8,128)(2,1)} %w_ref.3) | copy-start | bytes 14155780
  10.7 3.7 %copy-start.3 = (bf16[1,6,128,512]{3,2,1,0:T(8,128)(2,1)S(1)}, bf16[1,6,128,512]{3,2,1,0:T(8,128)(2,1)}, u32[]{:S(2)}) copy-start(bf16[1,6,128,512]{3,2,1,0:T(8,128)(2,1)} %param.11) | copy-start | bytes 2359300
  16.7 5.5 %copy-start.11 = (s32[1,6,4]{1,2,0:T(4,128)S(1)}, s32[1,6,4]{1,2,0:T(4,128)}, u32[]{:S(2)}) copy-start(s32[1,6,4]{1,2,0:T(4,128)} %param.20) | copy-start | bytes 292
  16.7 48.8 %copy-start.12 = (s32[1,6]{1,0:T(1,128)S(1)}, s32[1,6]{1,0:T(1,128)}, u32[]{:S(2)}) copy-start(s32[1,6]{1,0:T(1,128)} %param.21) | copy-start | bytes 76
  16.7 48.9 %copy-start.5 = (bf16[512,512]{1,0:T(8,128)(2,1)S(1)}, bf16[512,512]{1,0:T(8,128)(2,1)}, u32[]{:S(2)}) copy-start(bf16[512,512]{1,0:T(8,128)(2,1)} %wq_ref.1) | copy-start | bytes 1572868
  16.7 48.9 %copy-start.6 = (bf16[512,512]{1,0:T(8,128)(2,1)S(1)}, bf16[512,512]{1,0:T(8,128)(2,1)}, u32[]{:S(2)}) copy-start(bf16[512,512]{1,0:T(8,128)(2,1)} %wk_ref.3) | copy-start | bytes 1572868
  16.7 48.9 %copy-start.7 = (bf16[512,512]{1,0:T(8,128)(2,1)S(1)}, bf16[512,512]{1,0:T(8,128)(2,1)}, u32[]{:S(2)}) copy-start(bf16[512,512]{1,0:T(8,128)(2,1)} %wv_ref.3) | copy-start | bytes 1572868
  16.8 48.8 %copy-start.9 = (f32[512]{0:T(512)S(1)}, f32[512]{0:T(512)}, u32[]{:S(2)}) copy-start(f32[512]{0:T(512)} %param.18) | copy-start | bytes 6148
  16.8 48.8 %copy-start.10 = (f32[512]{0:T(512)S(1)}, f32[512]{0:T(512)}, u32[]{:S(2)}) copy-start(f32[512]{0:T(512)} %param.19) | copy-start | bytes 6148
  16.9 41.7 %collective-permute-start.2 = (bf16[768,512]{1,0:T(8,128)(2,1)S(1)}, bf16[768,512]{1,0:T(8,128)(2,1)S(1)}, u32[]{:S(2)}, u32[]{:S(2)}) collective-permute-start(bf16[768,512]{1,0:T(8,128)(2,1)S(1)} %pad_maximum_fusion.f_ref), channel_id=1, source_target_pairs={{0,16},{16,32},{32,48},{48,64},{64,80},{80,96},{96,112},{112,128},... | collective-permute-start | bytes 2359304 | tf_op jit(solution)/shard_map/ppermute | solution.py:230
  59.4 11.7 %collective-permute-start.4 = (bf16[256,512]{1,0:T(8,128)(2,1)}, bf16[256,512]{1,0:T(8,128)(2,1)S(1)}, u32[]{:S(2)}, u32[]{:S(2)}) collective-permute-start(bf16[256,512]{1,0:T(8,128)(2,1)} %get-tuple-element.11), channel_id=1, source_target_pairs={{1,0},{2,1},{3,2},{4,3},{5,4},{6,5},{7,6},{8,7},{9,8},{10,9},{11,1... | collective-permute-start | bytes 786440 | tf_op jit(solution)/shard_map/ppermute | solution.py:230
  63.5 10.1 %collective-permute-start.3 = (bf16[256,512]{1,0:T(8,128)(2,1)}, bf16[256,512]{1,0:T(8,128)(2,1)}, u32[]{:S(2)}, u32[]{:S(2)}) collective-permute-start(bf16[256,512]{1,0:T(8,128)(2,1)} %get-tuple-element.12), channel_id=1, source_target_pairs={{0,1},{1,2},{2,3},{3,4},{4,5},{5,6},{6,7},{7,8},{8,9},{9,10},{10,1... | collective-permute-start | bytes 786440 | tf_op jit(solution)/shard_map/ppermute | solution.py:230
  65.6 8.0 %copy-start.8 = (bf16[512,512]{1,0:T(8,128)(2,1)S(1)}, bf16[512,512]{1,0:T(8,128)(2,1)}, u32[]{:S(2)}) copy-start(bf16[512,512]{1,0:T(8,128)(2,1)} %wo_ref.1) | copy-start | bytes 1572868

commit v2 on v0

v2 whole, which is shorter than its diff:
```python
import jax
import jax.numpy as jnp
from jax import lax
from jax.experimental import pallas as pl
from jax.experimental.pallas import tpu as pltpu
from jax.sharding import PartitionSpec as P

HEADS = 8
HD = 64
KSRC = 4
BLOCK = 128
DISP = 2
PAIR = 2 * HD
VMEM_BYTES = 40 * 1024 * 1024

NT = (((1,), (1,)), ((), ()))


def dot(a, b):
    return jnp.dot(a, b, preferred_element_type=jnp.float32)


def from_left(y):
    column = lax.broadcasted_iota(jnp.int32, y.shape, 0) % BLOCK
    return jnp.where(column == 0, 0.0, pltpu.roll(y, 1, 0))


def from_right(y):
    column = lax.broadcasted_iota(jnp.int32, y.shape, 0) % BLOCK
    return jnp.where(column == BLOCK - 1, 0.0, pltpu.roll(y, y.shape[0] - 1, 0))


def row_of(index, count=1):
    return pl.ds(index * BLOCK, count * BLOCK)


def conv_inner_kernel(x_ref, w_hbm, b_ref, out_ref, w_ref, acc_ref, sems):
    rows = out_ref.shape[0] // BLOCK
    order = (1, 0, 2)
    copies = [
        pltpu.make_async_copy(w_hbm.at[:, c], w_ref.at[:, c], sems.at[c]) for c in range(3)
    ]
    for c in order:
        copies[c].start()
    for c in order:
        copies[c].wait()
        y = sum(dot(x_ref[row_of(a, rows)], w_ref[a, c]) for a in range(3))
        if c == 1:
            acc_ref[...] = y + b_ref[...]
        elif c == 0:
            acc_ref[...] += from_left(y)
        else:
            out_ref[...] = (acc_ref[...] + from_right(y)).astype(jnp.bfloat16)


def conv_edge_kernel(before_ref, x_ref, after_ref, inner_ref, w_ref, b_ref, outer_ref, mid_ref):
    rows = x_ref.shape[0] // BLOCK
    upper = [before_ref[...], x_ref[row_of(0)], x_ref[row_of(1)]]
    lower = [x_ref[row_of(rows - 2)], x_ref[row_of(rows - 1)], after_ref[...]]
    lines = [jnp.concatenate([upper[a], lower[a]], 0) for a in range(3)]
    left, mid, right = (sum(dot(lines[a], w_ref[a, c]) for a in range(3)) for c in range(3))
    total = from_left(left) + (mid + b_ref[...]) + from_right(right)
    total = total.astype(jnp.bfloat16)
    outer_ref[row_of(0)] = total[:BLOCK]
    outer_ref[row_of(2 * DISP - 1)] = total[BLOCK:]
    outer_ref[row_of(1, DISP - 1)] = inner_ref[row_of(0, DISP - 1)]
    outer_ref[row_of(DISP, DISP - 1)] = inner_ref[row_of(rows - 1 - DISP, DISP - 1)]
    mid_ref[...] = inner_ref[row_of(DISP - 1, rows - 2 * DISP)]


def head_norm(proj, gain):
    squares = (proj * proj).astype(jnp.bfloat16)
    wide = 4 * HD
    row = lax.broadcasted_iota(jnp.int32, (wide, wide), 0) // HD
    col = lax.broadcasted_iota(jnp.int32, (wide, wide), 1) // HD
    mean_of = jnp.where(row == col, 1.0 / HD, 0.0).astype(jnp.bfloat16)
    means = [dot(squares[:, i : i + wide], mean_of) for i in range(0, HEADS * HD, wide)]
    mean = jnp.concatenate(means, 1)
    return (proj * lax.rsqrt(mean + 1e-06) * gain).astype(jnp.bfloat16)


def pair_product(q, k, v, weights=None):
    low = lax.broadcasted_iota(jnp.int32, (BLOCK, PAIR), 1) < HD
    zero = jnp.zeros((BLOCK, PAIR), jnp.bfloat16)
    one = jnp.ones((BLOCK, PAIR), jnp.bfloat16)
    keys = jnp.concatenate([jnp.where(low, k, zero), jnp.where(low, zero, k)], 0)
    expo = jnp.exp(lax.dot_general(q, keys, NT, preferred_element_type=jnp.float32))
    if weights is not None:
        blocks = [expo[i * BLOCK : (i + 1) * BLOCK] * w for i, w in enumerate(weights)]
        expo = jnp.concatenate(blocks, 0)
    upper = jnp.concatenate([jnp.where(low, v, zero), jnp.where(low, one, zero)], 1)
    lower = jnp.concatenate([jnp.where(low, zero, v), jnp.where(low, zero, one)], 1)
    return dot(expo.astype(jnp.bfloat16), jnp.concatenate([upper, lower], 0))


def own_kernel(outer_ref, mid_ref, wq_ref, wk_ref, wv_ref, gq_ref, gk_ref, q_ref, acc_ref, k_ref, v_ref):
    reach = DISP * BLOCK
    inner = mid_ref.shape[0]
    pieces = ((outer_ref.at[:reach], 0), (mid_ref, reach), (outer_ref.at[reach:], reach + inner))
    for ref, start in pieces:
        feats = ref[...]
        rows = pl.ds(start, feats.shape[0])
        q_ref[rows] = head_norm(dot(feats, wq_ref[...]), gq_ref[...] * HD**-0.5)
        k_ref[rows] = head_norm(dot(feats, wk_ref[...]), gk_ref[...])
        v_ref[rows] = dot(feats, wv_ref[...]).astype(jnp.bfloat16)

    @pl.loop(0, q_ref.shape[0] // BLOCK)
    def _(block):
        rows = pl.ds(pl.multiple_of(block * BLOCK, BLOCK), BLOCK)
        for p in range(HEADS // 2):
            cols = pl.ds(p * PAIR, PAIR)
            acc_ref[rows, pl.ds(2 * p * PAIR, 2 * PAIR)] = pair_product(
                q_ref[rows, cols], k_ref[rows, cols], v_ref[rows, cols]
            )


def absorb(ids_ref, counts_ref, pieces, q_ref, acc_ref, wk_ref, wv_ref, gk_ref, k_ref, v_ref):
    rows = q_ref.shape[0] // BLOCK
    has_previous = lax.axis_index("frame") > 0
    first_row = lax.axis_index("row") * rows
    done = 0
    for ref, places in pieces:
        feats = ref[...]
        k_ref[row_of(done, len(places))] = head_norm(dot(feats, wk_ref[...]), gk_ref[...])
        v_ref[row_of(done, len(places))] = dot(feats, wv_ref[...]).astype(jnp.bfloat16)
        for i, place in enumerate(places):
            low, high = max(0, place - DISP), min(rows - 1, place + DISP)
            weights = []
            for r in range(low, high + 1):
                times = jnp.float32(0)
                for j in range(KSRC):
                    named = (ids_ref[r, j] == first_row + place) & (j < counts_ref[r]) & has_previous
                    times += jnp.where(named, jnp.float32(1), jnp.float32(0))
                weights.append(times)
            queries = row_of(low, high + 1 - low)
            source = row_of(done + i)
            for p in range(HEADS // 2):
                cols = pl.ds(p * PAIR, PAIR)
                acc_ref[queries, pl.ds(2 * p * PAIR, 2 * PAIR)] += pair_product(
                    q_ref[queries, cols], k_ref[source, cols], v_ref[source, cols], weights
                )
        done += len(places)


def outer_places(rows):
    return tuple(range(DISP)) + tuple(range(rows - DISP, rows))


def early_kernel(
    ids_ref, counts_ref, outer_ref, q_ref, acc_in_ref, wk_ref, wv_ref, gk_ref, acc_ref, k_ref, v_ref
):
    rows = q_ref.shape[0] // BLOCK
    acc_ref[...] = acc_in_ref[...]
    pieces = ((outer_ref, outer_places(rows)),)
    absorb(ids_ref, counts_ref, pieces, q_ref, acc_ref, wk_ref, wv_ref, gk_ref, k_ref, v_ref)


def halo_kernel(
    ids_ref, counts_ref, up_ref, down_ref, q_ref, acc_in_ref, wk_ref, wv_ref, gk_ref,
    acc_ref, k_ref, v_ref,
):
    rows = q_ref.shape[0] // BLOCK
    acc_ref[...] = acc_in_ref[...]
    pieces = ((up_ref, tuple(range(-DISP, 0))), (down_ref, tuple(range(rows, rows + DISP))))
    absorb(ids_ref, counts_ref, pieces, q_ref, acc_ref, wk_ref, wv_ref, gk_ref, k_ref, v_ref)


def late_kernel(
    ids_ref, counts_ref, mid_ref, q_ref, acc_in_ref, wk_ref, wv_ref, gk_ref,
    own_outer_ref, own_mid_ref, wo_ref, out_ref, acc_ref, k_ref, v_ref,
):
    rows = q_ref.shape[0] // BLOCK
    acc_ref[...] = acc_in_ref[...]
    pieces = ((mid_ref, tuple(range(DISP, rows - DISP))),)
    absorb(ids_ref, counts_ref, pieces, q_ref, acc_ref, wk_ref, wv_ref, gk_ref, k_ref, v_ref)
    parts = []
    for p in range(HEADS // 2):
        both = acc_ref[:, pl.ds(2 * p * PAIR, 2 * PAIR)]
        parts.append((both[:, :PAIR] / both[:, PAIR:]).astype(jnp.bfloat16))
    change = dot(jnp.concatenate(parts, 1), wo_ref[...])
    reach = DISP * BLOCK
    inner = own_mid_ref.shape[0]
    pieces = (
        (own_outer_ref.at[:reach], 0), (own_mid_ref, reach), (own_outer_ref.at[reach:], reach + inner),
    )
    for ref, start in pieces:
        feats = ref[...].astype(jnp.float32)
        stop = start + feats.shape[0]
        out_ref[start:stop] = (feats + change[start:stop]).astype(jnp.bfloat16)


SMEM = pl.BlockSpec(memory_space=pltpu.SMEM)
VMEM = pl.BlockSpec(memory_space=pltpu.VMEM)


def call(kernel, name, args, outs, scratch=(), specs=None, flops=0, aliases=None):
    moved = sum(a.size * a.dtype.itemsize for a in args)
    return pl.pallas_call(
        kernel,
        in_specs=specs or [VMEM] * len(args),
        out_specs=[VMEM] * len(outs),
        out_shape=[jax.ShapeDtypeStruct(shape, dtype) for shape, dtype in outs],
        scratch_shapes=list(scratch),
        input_output_aliases=aliases or {},
        compiler_params=pltpu.CompilerParams(vmem_limit_bytes=VMEM_BYTES),
        cost_estimate=pl.CostEstimate(flops=int(flops), bytes_accessed=int(moved), transcendentals=0),
        name=name,
    )(*args)


def passed_on(array, axis, distance):
    devices = range(lax.axis_size(axis))
    return lax.ppermute(array, axis, [(i, i + distance) for i in devices if i + distance in devices])


def shards(
    frames_x, conv_weight, conv_bias, query_weight, key_weight, value_weight, out_weight,
    query_gain, key_gain, source_ids, valid_counts,
):
    _, band_rows, width, chans = frames_x.shape
    tokens = band_rows * width
    reach = DISP * BLOCK
    x = frames_x.reshape(tokens, chans)
    bias = conv_bias.reshape(1, chans)
    gq = query_gain.reshape(1, chans)
    gk = key_gain.reshape(1, chans)
    ids, counts = source_ids[0], valid_counts[0]
    half, full = jnp.bfloat16, jnp.float32
    square = chans * chans

    before = passed_on(x[tokens - BLOCK :], "row", 1)
    after = passed_on(x[:BLOCK], "row", -1)
    (inner,) = call(
        conv_inner_kernel, "conv_inner", (x, conv_weight, bias), [((tokens - 2 * BLOCK, chans), half)],
        [
            pltpu.VMEM(conv_weight.shape, half),
            pltpu.VMEM((tokens - 2 * BLOCK, chans), full),
            pltpu.SemaphoreType.DMA((3,)),
        ],
        [VMEM, pl.BlockSpec(memory_space=pltpu.HBM), VMEM],
        18 * (tokens - 2 * BLOCK) * square,
    )
    outer, mid = call(
        conv_edge_kernel, "conv_edge", (before, x, after, inner, conv_weight, bias),
        [((2 * reach, chans), half), ((tokens - 2 * reach, chans), half)],
        flops=36 * BLOCK * square,
    )
    prev_outer = passed_on(outer, "frame", 1)
    prev_mid = passed_on(mid, "frame", 1)
    q, acc = call(
        own_kernel, "own_part", (outer, mid, query_weight, key_weight, value_weight, gq, gk),
        [((tokens, chans), half), ((tokens, 2 * chans), full)],
        [pltpu.VMEM((tokens, chans), half)] * 2,
        flops=10 * tokens * square,
    )
    prev_outer, q, acc = lax.optimization_barrier((prev_outer, q, acc))
    up = passed_on(prev_outer[reach:], "row", 1)
    down = passed_on(prev_outer[:reach], "row", -1)

    def keys_and_values(rows):
        return [pltpu.VMEM((rows * BLOCK, chans), half)] * 2

    weights = (key_weight, value_weight, gk)
    accs = [((tokens, 2 * chans), full)]
    (acc,) = call(
        early_kernel, "early_rows", (ids, counts, prev_outer, q, acc, *weights), accs,
        keys_and_values(2 * DISP), [SMEM] * 2 + [VMEM] * 6, 8 * tokens * square, {4: 0},
    )
    (acc,) = call(
        halo_kernel, "halo_rows", (ids, counts, up, down, q, acc, *weights), accs,
        keys_and_values(2 * DISP), [SMEM] * 2 + [VMEM] * 7, 4 * tokens * square, {5: 0},
    )
    (out,) = call(
        late_kernel, "late_rows", (ids, counts, prev_mid, q, acc, *weights, outer, mid, out_weight),
        [((tokens, chans), half)],
        [pltpu.VMEM((tokens, 2 * chans), full)] + keys_and_values(band_rows - 2 * DISP),
        [SMEM] * 2 + [VMEM] * 9, 8 * tokens * square,
    )
    return out.reshape(1, band_rows, width, chans)


def solution(mesh):
    return jax.shard_map(
        shards,
        mesh=mesh,
        in_specs=(
            P("frame", "row", None, None),
            P(), P(), P(), P(), P(), P(), P(), P(),
            P("frame", "row", None),
            P("frame", "row"),
        ),
        out_specs=P("frame", "row", None, None),
        check_vma=False,
    )
```

time: 186 us -> 75.9 us (0.41)
  the two profiles are of different devices: /device:TPU:57 before, /device:TPU:26 now
where the time goes in v2:
time: 75.9 us; the launch traced here: 75.4 us
  starting transfers between devices  25.7 us (34%)
  Pallas kernels  21.1 us (28%)
  waiting for transfers between devices  16.2 us (21%)
  local copies, waits for them, and re-layouts  12.1 us (16%)
    ppermute x6, starting transfers between devices, passed_on(): lax.ppermute(array, axis, [(i, i + distance) for i in devices if i + dist...  25.7 us
    pallas_call x6, Pallas kernels, call(): pl.pallas_call(kernel, in_specs=specs or [VMEM] * len(args), out_specs=[V...  21.1 us
    ppermute x6, waiting for transfers between devices, passed_on(): lax.ppermute(array, axis, [(i, i + distance) for i in devices if i + dist...  16.2 us
    unnamed x44, local copies, waits for them, and re-layouts  10.2 us
  transfers between devices with their start and end apart: 6, of which 2 were waited for; matrix products, arithmetic and copies ran while one was open for 0% of the time, Pallas kernels for 20%

profile of v2, /device:TPU:26, one launch (start us, length us, event | category | flops | bytes accessed | tf_op | source)
XLA Modules:
  0.0 75.4 jit_solution(7656404233584129701)
XLA Ops:
  0.0 1.0 %slice_bitcast_fusion = (bf16[128,512]{1,0:T(8,128)(2,1)S(1)}, bf16[128,512]{1,0:T(8,128)(2,1)S(1)}) fusion(bf16[1,6,128,512]{3,2,1,0:T(8,128)(2,1)} %param.11), kind=kLoop, calls=%fused_computation | loop fusion | bytes 524288 | tf_op jit(solution)/shard_map/slice | solution.py:232
  1.0 1.9 %collective-permute-start = (bf16[128,512]{1,0:T(8,128)(2,1)S(1)}, bf16[128,512]{1,0:T(8,128)(2,1)S(1)}, u32[]{:S(2)}, u32[]{:S(2)}) collective-permute-start(bf16[128,512]{1,0:T(8,128)(2,1)S(1)} %get-tuple-element.20), channel_id=1, source_target_pairs={{0,1},{1,2},{2,3},{3,4},{4,5},{5,6},{6,7},{7,8},{8,9},{9,10},{10,1... | collective-permute-start | bytes 393224 | tf_op jit(solution)/shard_map/ppermute | solution.py:213
  2.9 3.6 %collective-permute-start.1 = (bf16[128,512]{1,0:T(8,128)(2,1)S(1)}, bf16[128,512]{1,0:T(8,128)(2,1)S(1)}, u32[]{:S(2)}, u32[]{:S(2)}) collective-permute-start(bf16[128,512]{1,0:T(8,128)(2,1)S(1)} %get-tuple-element.19), channel_id=1, source_target_pairs={{1,0},{2,1},{3,2},{4,3},{5,4},{6,5},{7,6},{8,7},{9,8},{10,9},{11,1... | collective-permute-start | bytes 393224 | tf_op jit(solution)/shard_map/ppermute | solution.py:213
  6.6 0.0 copy-start.3
  6.6 2.3 %copy-done.3 = bf16[3,3,512,512]{3,2,1,0:T(8,128)(2,1)S(1)} copy-done((bf16[3,3,512,512]{3,2,1,0:T(8,128)(2,1)S(1)}, bf16[3,3,512,512]{3,2,1,0:T(8,128)(2,1)}, u32[]{:S(2)}) %copy-start.3) | copy-done | bytes 4718616
  8.9 1.1 %copy-done.12 = bf16[1,6,128,512]{3,2,1,0:T(8,128)(2,1)S(1)} copy-done((bf16[1,6,128,512]{3,2,1,0:T(8,128)(2,1)S(1)}, bf16[1,6,128,512]{3,2,1,0:T(8,128)(2,1)}, u32[]{:S(2)}) %copy-start.12) | copy-done | bytes 786456
  10.0 0.7 copy-done.18
  10.7 3.4 %conv_inner.1.inner_ref = bf16[512,512]{1,0:T(8,128)(2,1)S(1)} custom-call(bf16[768,512]{1,0:T(8,128)(2,1)S(1)} %bitcast.11, bf16[3,3,512,512]{3,2,1,0:T(8,128)(2,1)S(1)} %copy-done.3, f32[1,512]{1,0:T(1,128)S(1)} %bitcast.20), custom_call_target="tpu_custom_call" | custom-call | flops 2415919104 | bytes 5507072 | tf_op jit(solution)/shard_map/conv_inner/pallas_call | solution.py:198
  14.1 0.0 copy-start.4
  14.1 0.0 copy-start.7
  14.2 0.0 copy-start.16
  14.2 0.0 copy-start.19
  14.2 0.0 copy-start.20
  14.2 0.0 collective-permute-done.before_ref
  14.2 0.0 collective-permute-done.1.after_ref
  14.2 1.4 %conv_edge.1 = (bf16[512,512]{1,0:T(8,128)(2,1)S(1)}, bf16[256,512]{1,0:T(8,128)(2,1)S(1)}) custom-call(bf16[128,512]{1,0:T(8,128)(2,1)S(1)} %collective-permute-done.before_ref, bf16[768,512]{1,0:T(8,128)(2,1)S(1)} %bitcast.12, bf16[128,512]{1,0:T(8,128)(2,1)S(1)} %collective-permute-done.1.after_ref, bf16[512,512]{1,0:T(8,128)(2,1)S(1)} %conv_inner.1.inner_ref, ...), custom_call_target="tpu_custom_call" | custom-call | flops 1207959552 | bytes 6293504 | tf_op jit(solution)/shard_map/conv_edge/pallas_call | solution.py:198
  15.6 5.2 %collective-permute-start.3 = (bf16[512,512]{1,0:T(8,128)(2,1)S(1)}, bf16[512,512]{1,0:T(8,128)(2,1)S(1)}, u32[]{:S(2)}, u32[]{:S(2)}) collective-permute-start(bf16[512,512]{1,0:T(8,128)(2,1)S(1)} %get-tuple-element.13.outer_ref.own_outer_ref), channel_id=1, source_target_pairs={{0,16},{16,32},{32,48},{48,64},{64,80},{80,96},{96,112},{112,128},... | collective-permute-start | bytes 1572872 | tf_op jit(solution)/shard_map/ppermute | solution.py:213
  20.8 0.0 copy-done.4
  20.8 0.0 copy-done.7
  20.8 0.0 copy-done.16
  20.8 0.0 copy-done.19
  20.9 0.0 copy-done.20
  20.9 0.0 copy-start.21
  20.9 0.0 copy-start.17
  20.9 4.8 %own_part.1 = (bf16[768,512]{1,0:T(8,128)(2,1)S(1)}, f32[768,1024]{1,0:T(8,128)S(1)}) custom-call(bf16[512,512]{1,0:T(8,128)(2,1)S(1)} %get-tuple-element.13.outer_ref.own_outer_ref, bf16[256,512]{1,0:T(8,128)(2,1)S(1)} %get-tuple-element.12.mid_ref.own_mid_ref, bf16[512,512]{1,0:T(8,128)(2,1)S(1)} %copy-done.19, bf16[512,512]{1,0:T(8,128)(2,1)S(1)} %copy-done.4, ...), custom_call_target="tpu_custom_call" | custom-call | flops 2013265920 | bytes 2363392 | tf_op jit(solution)/shard_map/own_part/pallas_call | solution.py:198
  25.7 0.0 copy-start
  25.7 0.9 %copy-done = bf16[768,512]{1,0:T(8,128)(2,1)} copy-done((bf16[768,512]{1,0:T(8,128)(2,1)}, bf16[768,512]{1,0:T(8,128)(2,1)S(1)}, u32[]{:S(2)}) %copy-start) | copy-done | bytes 786456
  26.6 13.8 %collective-permute-done.3.outer_ref = bf16[512,512]{1,0:T(8,128)(2,1)S(1)} collective-permute-done((bf16[512,512]{1,0:T(8,128)(2,1)S(1)}, bf16[512,512]{1,0:T(8,128)(2,1)S(1)}, u32[]{:S(2)}, u32[]{:S(2)}) %collective-permute-start.3) | collective-permute-done | bytes 524320 | tf_op jit(solution)/shard_map/ppermute | solution.py:213
  40.4 0.8 %fusion = (bf16[256,512]{1,0:T(8,128)(2,1)}, bf16[256,512]{1,0:T(8,128)(2,1)}) fusion(bf16[512,512]{1,0:T(8,128)(2,1)S(1)} %collective-permute-done.3.outer_ref), kind=kLoop, calls=%fused_computation.2 | loop fusion | bytes 1048576 | tf_op jit(solution)/shard_map/slice | solution.py:258
  41.2 0.8 %copy-done.10 = bf16[512,512]{1,0:T(8,128)(2,1)} copy-done((bf16[512,512]{1,0:T(8,128)(2,1)}, bf16[512,512]{1,0:T(8,128)(2,1)S(1)}, u32[]{:S(2)}) %copy-start.10) | copy-done | bytes 524312
  42.0 1.9 %collective-permute-start.4 = (bf16[256,512]{1,0:T(8,128)(2,1)}, bf16[256,512]{1,0:T(8,128)(2,1)}, u32[]{:S(2)}, u32[]{:S(2)}) collective-permute-start(bf16[256,512]{1,0:T(8,128)(2,1)} %get-tuple-element.22), channel_id=1, source_target_pairs={{0,1},{1,2},{2,3},{3,4},{4,5},{5,6},{6,7},{7,8},{8,9},{9,10},{10,1... | collective-permute-start | bytes 786440 | tf_op jit(solution)/shard_map/ppermute | solution.py:213
  44.0 3.6 %collective-permute-start.5 = (bf16[256,512]{1,0:T(8,128)(2,1)}, bf16[256,512]{1,0:T(8,128)(2,1)}, u32[]{:S(2)}, u32[]{:S(2)}) collective-permute-start(bf16[256,512]{1,0:T(8,128)(2,1)} %get-tuple-element.21), channel_id=1, source_target_pairs={{1,0},{2,1},{3,2},{4,3},{5,4},{6,5},{7,6},{8,7},{9,8},{10,9},{11,1... | collective-permute-start | bytes 786440 | tf_op jit(solution)/shard_map/ppermute | solution.py:213
  47.6 9.4 %collective-permute-start.2 = (bf16[256,512]{1,0:T(8,128)(2,1)S(1)}, bf16[256,512]{1,0:T(8,128)(2,1)}, u32[]{:S(2)}, u32[]{:S(2)}) collective-permute-start(bf16[256,512]{1,0:T(8,128)(2,1)S(1)} %get-tuple-element.12.mid_ref.own_mid_ref), channel_id=1, source_target_pairs={{0,16},{16,32},{32,48},{48,64},{64,80},{80,96},{96,112},{112,128},... | collective-permute-start | bytes 786440 | tf_op jit(solution)/shard_map/ppermute | solution.py:213
  57.0 0.1 copy.16.ids_ref
  57.1 1.1 %copy-done.1 = bf16[768,512]{1,0:T(8,128)(2,1)S(1)} copy-done((bf16[768,512]{1,0:T(8,128)(2,1)S(1)}, bf16[768,512]{1,0:T(8,128)(2,1)}, u32[]{:S(2)}) %copy-start.1) | copy-done | bytes 786456
  58.2 1.0 %copy-done.5 = bf16[512,512]{1,0:T(8,128)(2,1)S(1)} copy-done((bf16[512,512]{1,0:T(8,128)(2,1)S(1)}, bf16[512,512]{1,0:T(8,128)(2,1)}, u32[]{:S(2)}) %copy-start.5) | copy-done | bytes 524312
  59.3 1.0 %copy-done.8 = bf16[512,512]{1,0:T(8,128)(2,1)S(1)} copy-done((bf16[512,512]{1,0:T(8,128)(2,1)S(1)}, bf16[512,512]{1,0:T(8,128)(2,1)}, u32[]{:S(2)}) %copy-start.8) | copy-done | bytes 524312
  60.3 1.0 %copy-done.11 = bf16[512,512]{1,0:T(8,128)(2,1)S(1)} copy-done((bf16[512,512]{1,0:T(8,128)(2,1)S(1)}, bf16[512,512]{1,0:T(8,128)(2,1)}, u32[]{:S(2)}) %copy-start.11) | copy-done | bytes 524312
  61.4 3.7 %early_rows.1.acc_in_ref = f32[768,1024]{1,0:T(8,128)S(1)} custom-call(s32[6,4]{1,0:T(8,128)S(1)} %copy.16.ids_ref, s32[6]{0:T(128)S(1)} %bitcast.17, bf16[512,512]{1,0:T(8,128)(2,1)S(1)} %copy-done.11, bf16[768,512]{1,0:T(8,128)(2,1)S(1)} %copy-done.1, f32[768,1024]{1,0:T(8,128)S(1)} %get-tuple-element.18.acc_in_ref, ...), custom_call_target="tpu_custom_call", output_to_operand_aliasing={{}: (4, {})} | custom-call | flops 1610612736 | bytes 5507192 | tf_op jit(solution)/shard_map/early_rows/pallas_call | solution.py:198
  65.0 0.0 copy-start.2
  65.0 0.0 copy-start.6
  65.1 0.0 copy-start.9
  65.1 0.0 copy-start.13
  65.1 0.0 collective-permute-done.4.up_ref
  65.1 0.0 collective-permute-done.5.down_ref
  65.1 3.4 %halo_rows.1.acc_in_ref = f32[768,1024]{1,0:T(8,128)S(1)} custom-call(s32[6,4]{1,0:T(8,128)S(1)} %copy.16.ids_ref, s32[6]{0:T(128)S(1)} %bitcast.18, bf16[256,512]{1,0:T(8,128)(2,1)} %collective-permute-done.4.up_ref, bf16[256,512]{1,0:T(8,128)(2,1)} %collective-permute-done.5.down_ref, ...), custom_call_target="tpu_custom_call", output_to_operand_aliasing={{}: (5, {})} | custom-call | flops 805306368 | bytes 5507192 | tf_op jit(solution)/shard_map/halo_rows/pallas_call | solution.py:198
  68.5 2.4 %collective-permute-done.2.mid_ref = bf16[256,512]{1,0:T(8,128)(2,1)} collective-permute-done((bf16[256,512]{1,0:T(8,128)(2,1)S(1)}, bf16[256,512]{1,0:T(8,128)(2,1)}, u32[]{:S(2)}, u32[]{:S(2)}) %collective-permute-start.2) | collective-permute-done | bytes 262176 | tf_op jit(solution)/shard_map/ppermute | solution.py:213
  71.0 4.4 %late_rows.1 = bf16[768,512]{1,0:T(8,128)(2,1)} custom-call(s32[6,4]{1,0:T(8,128)S(1)} %copy.16.ids_ref, s32[6]{0:T(128)S(1)} %bitcast.19, bf16[256,512]{1,0:T(8,128)(2,1)} %collective-permute-done.2.mid_ref, bf16[768,512]{1,0:T(8,128)(2,1)S(1)} %copy-done.2, f32[768,1024]{1,0:T(8,128)S(1)} %halo_rows.1.acc_in_ref, bf16[512,512]{1,0:T(8,128)(2,1)S(1)} %copy-done.6, ...), custom_call_target="tpu_custom_call" | custom-call | flops 1610612736 | bytes 6555768 | tf_op jit(solution)/shard_map/late_rows/pallas_call | solution.py:198
  (17 shorter events, 0.0 us)
Async XLA Ops:
  1.0 13.2 %collective-permute-start = (bf16[128,512]{1,0:T(8,128)(2,1)S(1)}, bf16[128,512]{1,0:T(8,128)(2,1)S(1)}, u32[]{:S(2)}, u32[]{:S(2)}) collective-permute-start(bf16[128,512]{1,0:T(8,128)(2,1)S(1)} %get-tuple-element.20), channel_id=1, source_target_pairs={{0,1},{1,2},{2,3},{3,4},{4,5},{5,6},{6,7},{7,8},{8,9},{9,10},{10,1... | collective-permute-start | bytes 393224 | tf_op jit(solution)/shard_map/ppermute | solution.py:213
  2.9 11.3 %collective-permute-start.1 = (bf16[128,512]{1,0:T(8,128)(2,1)S(1)}, bf16[128,512]{1,0:T(8,128)(2,1)S(1)}, u32[]{:S(2)}, u32[]{:S(2)}) collective-permute-start(bf16[128,512]{1,0:T(8,128)(2,1)S(1)} %get-tuple-element.19), channel_id=1, source_target_pairs={{1,0},{2,1},{3,2},{4,3},{5,4},{6,5},{7,6},{8,7},{9,8},{10,9},{11,1... | collective-permute-start | bytes 393224 | tf_op jit(solution)/shard_map/ppermute | solution.py:213
  6.6 2.3 %copy-start.3 = (bf16[3,3,512,512]{3,2,1,0:T(8,128)(2,1)S(1)}, bf16[3,3,512,512]{3,2,1,0:T(8,128)(2,1)}, u32[]{:S(2)}) copy-start(bf16[3,3,512,512]{3,2,1,0:T(8,128)(2,1)} %w_ref.1) | copy-start | bytes 14155780
  8.9 1.1 %copy-start.12 = (bf16[1,6,128,512]{3,2,1,0:T(8,128)(2,1)S(1)}, bf16[1,6,128,512]{3,2,1,0:T(8,128)(2,1)}, u32[]{:S(2)}) copy-start(bf16[1,6,128,512]{3,2,1,0:T(8,128)(2,1)} %param.11) | copy-start | bytes 2359300
  10.0 0.7 copy-start.18
  14.1 6.7 %copy-start.4 = (bf16[512,512]{1,0:T(8,128)(2,1)S(1)}, bf16[512,512]{1,0:T(8,128)(2,1)}, u32[]{:S(2)}) copy-start(bf16[512,512]{1,0:T(8,128)(2,1)} %wk_ref.7) | copy-start | bytes 1572868
  14.1 6.7 %copy-start.7 = (bf16[512,512]{1,0:T(8,128)(2,1)S(1)}, bf16[512,512]{1,0:T(8,128)(2,1)}, u32[]{:S(2)}) copy-start(bf16[512,512]{1,0:T(8,128)(2,1)} %wv_ref.7) | copy-start | bytes 1572868
  14.2 6.7 %copy-start.16 = (f32[512]{0:T(512)S(1)}, f32[512]{0:T(512)}, u32[]{:S(2)}) copy-start(f32[512]{0:T(512)} %param.19) | copy-start | bytes 6148
  14.2 6.7 %copy-start.19 = (bf16[512,512]{1,0:T(8,128)(2,1)S(1)}, bf16[512,512]{1,0:T(8,128)(2,1)}, u32[]{:S(2)}) copy-start(bf16[512,512]{1,0:T(8,128)(2,1)} %wq_ref.1) | copy-start | bytes 1572868
  14.2 6.7 %copy-start.20 = (f32[512]{0:T(512)S(1)}, f32[512]{0:T(512)}, u32[]{:S(2)}) copy-start(f32[512]{0:T(512)} %param.18) | copy-start | bytes 6148
  15.6 10.1 %copy-start.14 = (bf16[512,512]{1,0:T(8,128)(2,1)}, bf16[512,512]{1,0:T(8,128)(2,1)S(1)}, u32[]{:S(2)}) copy-start(bf16[512,512]{1,0:T(8,128)(2,1)S(1)} %get-tuple-element.13.outer_ref.own_outer_ref) | copy-start | bytes 1572868
  15.6 24.7 %collective-permute-start.3 = (bf16[512,512]{1,0:T(8,128)(2,1)S(1)}, bf16[512,512]{1,0:T(8,128)(2,1)S(1)}, u32[]{:S(2)}, u32[]{:S(2)}) collective-permute-start(bf16[512,512]{1,0:T(8,128)(2,1)S(1)} %get-tuple-element.13.outer_ref.own_outer_ref), channel_id=1, source_target_pairs={{0,16},{16,32},{32,48},{48,64},{64,80},{80,96},{96,112},{112,128},... | collective-permute-start | bytes 1572872 | tf_op jit(solution)/shard_map/ppermute | solution.py:213
  20.9 36.1 %copy-start.21 = (s32[1,6,4]{1,2,0:T(4,128)S(1)}, s32[1,6,4]{1,2,0:T(4,128)}, u32[]{:S(2)}) copy-start(s32[1,6,4]{1,2,0:T(4,128)} %param.20) | copy-start | bytes 292
  20.9 36.2 %copy-start.17 = (s32[1,6]{1,0:T(1,128)S(1)}, s32[1,6]{1,0:T(1,128)}, u32[]{:S(2)}) copy-start(s32[1,6]{1,0:T(1,128)} %param.21) | copy-start | bytes 76
  25.7 0.9 %copy-start = (bf16[768,512]{1,0:T(8,128)(2,1)}, bf16[768,512]{1,0:T(8,128)(2,1)S(1)}, u32[]{:S(2)}) copy-start(bf16[768,512]{1,0:T(8,128)(2,1)S(1)} %get-tuple-element.16.q_ref) | copy-start | bytes 2359300
  41.2 0.8 %copy-start.10 = (bf16[512,512]{1,0:T(8,128)(2,1)}, bf16[512,512]{1,0:T(8,128)(2,1)S(1)}, u32[]{:S(2)}) copy-start(bf16[512,512]{1,0:T(8,128)(2,1)S(1)} %collective-permute-done.3.outer_ref) | copy-start | bytes 1572868
  42.0 23.1 %collective-permute-start.4 = (bf16[256,512]{1,0:T(8,128)(2,1)}, bf16[256,512]{1,0:T(8,128)(2,1)}, u32[]{:S(2)}, u32[]{:S(2)}) collective-permute-start(bf16[256,512]{1,0:T(8,128)(2,1)} %get-tuple-element.22), channel_id=1, source_target_pairs={{0,1},{1,2},{2,3},{3,4},{4,5},{5,6},{6,7},{7,8},{8,9},{9,10},{10,1... | collective-permute-start | bytes 786440 | tf_op jit(solution)/shard_map/ppermute | solution.py:213
  44.0 21.2 %collective-permute-start.5 = (bf16[256,512]{1,0:T(8,128)(2,1)}, bf16[256,512]{1,0:T(8,128)(2,1)}, u32[]{:S(2)}, u32[]{:S(2)}) collective-permute-start(bf16[256,512]{1,0:T(8,128)(2,1)} %get-tuple-element.21), channel_id=1, source_target_pairs={{1,0},{2,1},{3,2},{4,3},{5,4},{6,5},{7,6},{8,7},{9,8},{10,9},{11,1... | collective-permute-start | bytes 786440 | tf_op jit(solution)/shard_map/ppermute | solution.py:213
  47.6 23.3 %collective-permute-start.2 = (bf16[256,512]{1,0:T(8,128)(2,1)S(1)}, bf16[256,512]{1,0:T(8,128)(2,1)}, u32[]{:S(2)}, u32[]{:S(2)}) collective-permute-start(bf16[256,512]{1,0:T(8,128)(2,1)S(1)} %get-tuple-element.12.mid_ref.own_mid_ref), channel_id=1, source_target_pairs={{0,16},{16,32},{32,48},{48,64},{64,80},{80,96},{96,112},{112,128},... | collective-permute-start | bytes 786440 | tf_op jit(solution)/shard_map/ppermute | solution.py:213
  57.1 1.1 %copy-start.1 = (bf16[768,512]{1,0:T(8,128)(2,1)S(1)}, bf16[768,512]{1,0:T(8,128)(2,1)}, u32[]{:S(2)}) copy-start(bf16[768,512]{1,0:T(8,128)(2,1)} %copy-done) | copy-start | bytes 2359300
  58.2 1.0 %copy-start.5 = (bf16[512,512]{1,0:T(8,128)(2,1)S(1)}, bf16[512,512]{1,0:T(8,128)(2,1)}, u32[]{:S(2)}) copy-start(bf16[512,512]{1,0:T(8,128)(2,1)} %wk_ref.7) | copy-start | bytes 1572868
  59.3 1.0 %copy-start.8 = (bf16[512,512]{1,0:T(8,128)(2,1)S(1)}, bf16[512,512]{1,0:T(8,128)(2,1)}, u32[]{:S(2)}) copy-start(bf16[512,512]{1,0:T(8,128)(2,1)} %wv_ref.7) | copy-start | bytes 1572868
  60.3 1.0 %copy-start.11 = (bf16[512,512]{1,0:T(8,128)(2,1)S(1)}, bf16[512,512]{1,0:T(8,128)(2,1)}, u32[]{:S(2)}) copy-start(bf16[512,512]{1,0:T(8,128)(2,1)} %copy-done.10) | copy-start | bytes 1572868
  65.0 5.9 %copy-start.2 = (bf16[768,512]{1,0:T(8,128)(2,1)S(1)}, bf16[768,512]{1,0:T(8,128)(2,1)}, u32[]{:S(2)}) copy-start(bf16[768,512]{1,0:T(8,128)(2,1)} %copy-done) | copy-start | bytes 2359300
  65.0 5.9 %copy-start.6 = (bf16[512,512]{1,0:T(8,128)(2,1)S(1)}, bf16[512,512]{1,0:T(8,128)(2,1)}, u32[]{:S(2)}) copy-start(bf16[512,512]{1,0:T(8,128)(2,1)} %wk_ref.7) | copy-start | bytes 1572868
  65.1 5.9 %copy-start.9 = (bf16[512,512]{1,0:T(8,128)(2,1)S(1)}, bf16[512,512]{1,0:T(8,128)(2,1)}, u32[]{:S(2)}) copy-start(bf16[512,512]{1,0:T(8,128)(2,1)} %wv_ref.7) | copy-start | bytes 1572868
  65.1 5.9 %copy-start.13 = (bf16[512,512]{1,0:T(8,128)(2,1)S(1)}, bf16[512,512]{1,0:T(8,128)(2,1)}, u32[]{:S(2)}) copy-start(bf16[512,512]{1,0:T(8,128)(2,1)} %wo_ref.1) | copy-start | bytes 1572868
  65.1 5.9 %copy-start.15 = (bf16[512,512]{1,0:T(8,128)(2,1)S(1)}, bf16[512,512]{1,0:T(8,128)(2,1)}, u32[]{:S(2)}) copy-start(bf16[512,512]{1,0:T(8,128)(2,1)} %copy-done.14) | copy-start | bytes 1572868

commit v3 on v2

v3 whole, which is shorter than its diff:
```python
import jax
import jax.numpy as jnp
from jax import lax
from jax.experimental import pallas as pl
from jax.experimental.pallas import tpu as pltpu
from jax.sharding import PartitionSpec as P

HEADS = 8
HD = 64
KSRC = 4
BLOCK = 128
DISP = 2
PAIR = 2 * HD

NT = (((1,), (1,)), ((), ()))


def dot(a, b):
    return jnp.dot(a, b, preferred_element_type=jnp.float32)


def from_left(y):
    column = lax.broadcasted_iota(jnp.int32, y.shape, 0) % BLOCK
    return jnp.where(column == 0, 0.0, pltpu.roll(y, 1, 0))


def from_right(y):
    column = lax.broadcasted_iota(jnp.int32, y.shape, 0) % BLOCK
    return jnp.where(column == BLOCK - 1, 0.0, pltpu.roll(y, y.shape[0] - 1, 0))


def row_of(index, count=1):
    return pl.ds(index * BLOCK, count * BLOCK)


def convolved(lines, w_ref, b_ref):
    left, mid, right = (sum(dot(lines(a), w_ref[a, c]) for a in range(3)) for c in range(3))
    return (from_left(left) + (mid + b_ref[...]) + from_right(right)).astype(jnp.bfloat16)


def conv_mid_kernel(x_ref, w_ref, b_ref, first_ref, last_ref, mid_ref):
    rows = mid_ref.shape[0] // BLOCK
    first_ref[...] = x_ref[row_of(0)]
    last_ref[...] = x_ref[row_of(rows + 2 * DISP - 1)]
    mid_ref[...] = convolved(lambda a: x_ref[row_of(DISP - 1 + a, rows)], w_ref, b_ref)


def conv_edge_kernel(before_ref, x_ref, after_ref, w_ref, b_ref, top_ref, bottom_ref):
    rows = x_ref.shape[0] // BLOCK
    held = DISP + 1
    upper = jnp.concatenate([before_ref[...], x_ref[row_of(0, held)]], 0)
    lower = jnp.concatenate([x_ref[row_of(rows - held, held)], after_ref[...]], 0)

    def lines(a):
        part = slice(a * BLOCK, (a + DISP) * BLOCK)
        return jnp.concatenate([upper[part], lower[part]], 0)

    total = convolved(lines, w_ref, b_ref)
    top_ref[...] = total[: DISP * BLOCK]
    bottom_ref[...] = total[DISP * BLOCK :]


def head_norm(proj, gain):
    squares = (proj * proj).astype(jnp.bfloat16)
    wide = 4 * HD
    row = lax.broadcasted_iota(jnp.int32, (wide, wide), 0) // HD
    col = lax.broadcasted_iota(jnp.int32, (wide, wide), 1) // HD
    mean_of = jnp.where(row == col, 1.0 / HD, 0.0).astype(jnp.bfloat16)
    means = [dot(squares[:, i : i + wide], mean_of) for i in range(0, HEADS * HD, wide)]
    mean = jnp.concatenate(means, 1)
    return (proj * lax.rsqrt(mean + 1e-06) * gain).astype(jnp.bfloat16)


def pair_product(q, k, v, weights=None):
    low = lax.broadcasted_iota(jnp.int32, (BLOCK, PAIR), 1) < HD
    zero = jnp.zeros((BLOCK, PAIR), jnp.bfloat16)
    one = jnp.ones((BLOCK, PAIR), jnp.bfloat16)
    keys = jnp.concatenate([jnp.where(low, k, zero), jnp.where(low, zero, k)], 0)
    expo = jnp.exp(lax.dot_general(q, keys, NT, preferred_element_type=jnp.float32))
    if weights is not None:
        blocks = [expo[i * BLOCK : (i + 1) * BLOCK] * w for i, w in enumerate(weights)]
        expo = jnp.concatenate(blocks, 0)
    upper = jnp.concatenate([jnp.where(low, v, zero), jnp.where(low, one, zero)], 1)
    lower = jnp.concatenate([jnp.where(low, zero, v), jnp.where(low, zero, one)], 1)
    return dot(expo.astype(jnp.bfloat16), jnp.concatenate([upper, lower], 0))


def band_pieces(top_ref, mid_ref, bottom_ref):
    reach = DISP * BLOCK
    return ((top_ref, 0), (mid_ref, reach), (bottom_ref, reach + mid_ref.shape[0]))


def own_kernel(
    top_ref, mid_ref, bottom_ref, wq_ref, wk_ref, wv_ref, gq_ref, gk_ref, q_ref, acc_ref, k_ref, v_ref
):
    pieces = band_pieces(top_ref, mid_ref, bottom_ref)
    for ref, start in pieces:
        feats = ref[...]
        rows = pl.ds(start, feats.shape[0])
        q_ref[rows] = head_norm(dot(feats, wq_ref[...]), gq_ref[...] * HD**-0.5)
        k_ref[rows] = head_norm(dot(feats, wk_ref[...]), gk_ref[...])
        v_ref[rows] = dot(feats, wv_ref[...]).astype(jnp.bfloat16)

    @pl.loop(0, q_ref.shape[0] // BLOCK)
    def _(block):
        rows = pl.ds(pl.multiple_of(block * BLOCK, BLOCK), BLOCK)
        for p in range(HEADS // 2):
            cols = pl.ds(p * PAIR, PAIR)
            acc_ref[rows, pl.ds(2 * p * PAIR, 2 * PAIR)] = pair_product(
                q_ref[rows, cols], k_ref[rows, cols], v_ref[rows, cols]
            )


def absorb(ids_ref, counts_ref, pieces, q_ref, acc_ref, wk_ref, wv_ref, gk_ref, k_ref, v_ref, base=0):
    rows = q_ref.shape[0] // BLOCK
    has_previous = lax.axis_index("frame") > 0
    first_row = lax.axis_index("row") * rows
    done = 0
    for ref, places in pieces:
        feats = ref[...]
        k_ref[row_of(done, len(places))] = head_norm(dot(feats, wk_ref[...]), gk_ref[...])
        v_ref[row_of(done, len(places))] = dot(feats, wv_ref[...]).astype(jnp.bfloat16)
        for i, place in enumerate(places):
            low, high = max(0, place - DISP), min(rows - 1, place + DISP)
            weights = []
            for r in range(low, high + 1):
                times = jnp.float32(0)
                for j in range(KSRC):
                    named = (ids_ref[r, j] == first_row + place) & (j < counts_ref[r]) & has_previous
                    times += jnp.where(named, jnp.float32(1), jnp.float32(0))
                weights.append(times)
            queries = row_of(low, high + 1 - low)
            sums = row_of(low - base, high + 1 - low)
            source = row_of(done + i)
            for p in range(HEADS // 2):
                cols = pl.ds(p * PAIR, PAIR)
                acc_ref[sums, pl.ds(2 * p * PAIR, 2 * PAIR)] += pair_product(
                    q_ref[queries, cols], k_ref[source, cols], v_ref[source, cols], weights
                )
        done += len(places)


def mid_kernel(
    ids_ref, counts_ref, prev_ref, q_ref, acc_in_ref, wk_ref, wv_ref, gk_ref, acc_ref, k_ref, v_ref
):
    rows = q_ref.shape[0] // BLOCK
    acc_ref[...] = acc_in_ref[...]
    pieces = ((prev_ref, tuple(range(DISP, rows - DISP))),)
    absorb(ids_ref, counts_ref, pieces, q_ref, acc_ref, wk_ref, wv_ref, gk_ref, k_ref, v_ref)


def top_kernel(
    ids_ref, counts_ref, prev_ref, q_ref, acc_in_ref, wk_ref, wv_ref, gk_ref, acc_ref, k_ref, v_ref
):
    acc_ref[...] = acc_in_ref[...]
    pieces = ((prev_ref, tuple(range(DISP))),)
    absorb(ids_ref, counts_ref, pieces, q_ref, acc_ref, wk_ref, wv_ref, gk_ref, k_ref, v_ref)


def finish(acc_ref, wo_ref, pieces, out_ref):
    parts = []
    for p in range(HEADS // 2):
        both = acc_ref[:, pl.ds(2 * p * PAIR, 2 * PAIR)]
        parts.append((both[:, :PAIR] / both[:, PAIR:]).astype(jnp.bfloat16))
    change = dot(jnp.concatenate(parts, 1), wo_ref[...])
    begin = 0
    for ref in pieces:
        feats = ref[...].astype(jnp.float32)
        stop = begin + feats.shape[0]
        out_ref[begin:stop] = (feats + change[begin:stop]).astype(jnp.bfloat16)
        begin = stop


def bottom_kernel(
    ids_ref, counts_ref, prev_ref, below_ref, q_ref, acc_in_ref, wk_ref, wv_ref, gk_ref,
    mid_ref, bottom_ref, wo_ref, out_hbm, acc_ref, k_ref, v_ref, out_ref, sem,
):
    rows = q_ref.shape[0] // BLOCK
    acc_ref[...] = acc_in_ref[DISP * BLOCK :]
    pieces = ((prev_ref, tuple(range(rows - DISP, rows))), (below_ref, tuple(range(rows, rows + DISP))))
    absorb(ids_ref, counts_ref, pieces, q_ref, acc_ref, wk_ref, wv_ref, gk_ref, k_ref, v_ref, DISP)
    finish(acc_ref, wo_ref, (mid_ref, bottom_ref), out_ref)
    copy = pltpu.make_async_copy(out_ref, out_hbm.at[row_of(DISP, rows - DISP)], sem)
    copy.start()
    copy.wait()


def last_kernel(
    ids_ref, counts_ref, above_ref, q_ref, acc_in_ref, wk_ref, wv_ref, gk_ref,
    top_ref, wo_ref, rest_hbm, out_hbm, acc_ref, k_ref, v_ref, out_ref, sem,
):
    del rest_hbm
    acc_ref[...] = acc_in_ref[: DISP * BLOCK]
    pieces = ((above_ref, tuple(range(-DISP, 0))),)
    absorb(ids_ref, counts_ref, pieces, q_ref, acc_ref, wk_ref, wv_ref, gk_ref, k_ref, v_ref)
    finish(acc_ref, wo_ref, (top_ref,), out_ref)
    copy = pltpu.make_async_copy(out_ref, out_hbm.at[row_of(0, DISP)], sem)
    copy.start()
    copy.wait()


SMEM = pl.BlockSpec(memory_space=pltpu.SMEM)
VMEM = pl.BlockSpec(memory_space=pltpu.VMEM)


HBM = pl.BlockSpec(memory_space=pltpu.HBM)
MEBI = 1024 * 1024


def call(kernel, name, args, outs, scratch=(), specs=None, aliases=None, limit=24, cost=2, out_specs=None):
    return pl.pallas_call(
        kernel,
        in_specs=specs or [VMEM] * len(args),
        out_specs=out_specs or [VMEM] * len(outs),
        out_shape=[jax.ShapeDtypeStruct(shape, dtype) for shape, dtype in outs],
        scratch_shapes=list(scratch),
        input_output_aliases=aliases or {},
        compiler_params=pltpu.CompilerParams(vmem_limit_bytes=limit * MEBI),
        cost_estimate=pl.CostEstimate(flops=cost * 1000000000, bytes_accessed=0, transcendentals=0),
        name=name,
    )(*args)


def passed_on(array, axis, distance):
    devices = range(lax.axis_size(axis))
    return lax.ppermute(array, axis, [(i, i + distance) for i in devices if i + distance in devices])


def shards(
    frames_x, conv_weight, conv_bias, query_weight, key_weight, value_weight, out_weight,
    query_gain, key_gain, source_ids, valid_counts,
):
    _, band_rows, width, chans = frames_x.shape
    tokens = band_rows * width
    reach = DISP * BLOCK
    x = frames_x.reshape(tokens, chans)
    bias = conv_bias.reshape(1, chans)
    gq = query_gain.reshape(1, chans)
    gk = key_gain.reshape(1, chans)
    ids, counts = source_ids[0], valid_counts[0]
    half, full = jnp.bfloat16, jnp.float32
    dma = pltpu.SemaphoreType.DMA

    first, last, mid = call(
        conv_mid_kernel, "conv_mid", (x, conv_weight, bias),
        [((BLOCK, chans), half), ((BLOCK, chans), half), ((tokens - 2 * reach, chans), half)],
        cost=2,
    )
    before = passed_on(last, "row", 1)
    after = passed_on(first, "row", -1)
    top, bottom = call(
        conv_edge_kernel, "conv_edge", (before, x, after, conv_weight, bias),
        [((reach, chans), half)] * 2,
        cost=0,
    )
    prev_mid = passed_on(mid, "frame", 1)
    prev_top = passed_on(top, "frame", 1)
    q, acc = call(
        own_kernel, "own_part", (top, mid, bottom, query_weight, key_weight, value_weight, gq, gk),
        [((tokens, chans), half), ((tokens, 2 * chans), full)],
        [pltpu.VMEM((tokens, chans), half)] * 2,
    )
    bottom, q = lax.optimization_barrier((bottom, q))
    prev_bottom = passed_on(bottom, "frame", 1)

    def keys_and_values(rows):
        return [pltpu.VMEM((rows * BLOCK, chans), half)] * 2

    weights = (key_weight, value_weight, gk)
    accs = [((tokens, 2 * chans), full)]
    (acc,) = call(
        mid_kernel, "mid_rows", (ids, counts, prev_mid, q, acc, *weights), accs,
        keys_and_values(band_rows - 2 * DISP), [SMEM] * 2 + [VMEM] * 6, {4: 0}, cost=40,
    )
    prev_top, acc = lax.optimization_barrier((prev_top, acc))
    below = passed_on(prev_top, "row", -1)
    (acc,) = call(
        top_kernel, "top_rows", (ids, counts, prev_top, q, acc, *weights), accs,
        keys_and_values(DISP), [SMEM] * 2 + [VMEM] * 6, {4: 0},
    )
    prev_bottom, acc = lax.optimization_barrier((prev_bottom, acc))
    above = passed_on(prev_bottom, "row", 1)
    outs = [((tokens, chans), half)]
    (out,) = call(
        bottom_kernel, "bottom_rows",
        (ids, counts, prev_bottom, below, q, acc, *weights, mid, bottom, out_weight), outs,
        [pltpu.VMEM((tokens - reach, 2 * chans), full)] + keys_and_values(2 * DISP)
        + [pltpu.VMEM((tokens - reach, chans), half), dma(())],
        [SMEM] * 2 + [VMEM] * 10, out_specs=[HBM],
    )
    (out,) = call(
        last_kernel, "last_rows", (ids, counts, above, q, acc, *weights, top, out_weight, out), outs,
        [pltpu.VMEM((reach, 2 * chans), full)] + keys_and_values(DISP)
        + [pltpu.VMEM((reach, chans), half), dma(())],
        [SMEM] * 2 + [VMEM] * 8 + [HBM], {10: 0}, out_specs=[HBM],
    )
    return out.reshape(1, band_rows, width, chans)


def solution(mesh):
    return jax.shard_map(
        shards,
        mesh=mesh,
        in_specs=(
            P("frame", "row", None, None),
            P(), P(), P(), P(), P(), P(), P(), P(),
            P("frame", "row", None),
            P("frame", "row"),
        ),
        out_specs=P("frame", "row", None, None),
        check_vma=False,
    )
```

time: 75.9 us -> 66.5 us (0.88)
  the two profiles are of different devices: /device:TPU:26 before, /device:TPU:57 now
where the time goes in v3:
time: 66.5 us; the launch traced here: 66.1 us
  starting transfers between devices  32.5 us (49%)
  Pallas kernels  21.1 us (32%)
  local copies, waits for them, and re-layouts  6.62 us (10%)
  waiting for transfers between devices  5.45 us (8%)
    ppermute x7, starting transfers between devices, passed_on(): lax.ppermute(array, axis, [(i, i + distance) for i in devices if i + dist...  32.5 us
    pallas_call x7, Pallas kernels, call(): pl.pallas_call(kernel, in_specs=specs or [VMEM] * len(args), out_specs=ou...  21.1 us
    unnamed x28, local copies, waits for them, and re-layouts  6.53 us
    ppermute x7, waiting for transfers between devices, passed_on(): lax.ppermute(array, axis, [(i, i + distance) for i in devices if i + dist...  5.45 us
  transfers between devices with their start and end apart: 7, of which 2 were waited for; matrix products, arithmetic and copies ran while one was open for 0% of the time, Pallas kernels for 26%

profile of v3, /device:TPU:57, one launch (start us, length us, event | category | flops | bytes accessed | tf_op | source)
XLA Modules:
  0.0 66.1 jit_solution(15796530797411475760)
XLA Ops:
  0.0 0.0 copy-start
  0.0 2.3 %copy-done = bf16[3,3,512,512]{3,2,1,0:T(8,128)(2,1)S(1)} copy-done((bf16[3,3,512,512]{3,2,1,0:T(8,128)(2,1)S(1)}, bf16[3,3,512,512]{3,2,1,0:T(8,128)(2,1)}, u32[]{:S(2)}) %copy-start) | copy-done | bytes 4718616
  2.3 0.0 copy-start.4
  2.3 1.1 %copy-done.4 = bf16[1,6,128,512]{3,2,1,0:T(8,128)(2,1)S(1)} copy-done((bf16[1,6,128,512]{3,2,1,0:T(8,128)(2,1)S(1)}, bf16[1,6,128,512]{3,2,1,0:T(8,128)(2,1)}, u32[]{:S(2)}) %copy-start.4) | copy-done | bytes 786456
  3.5 0.0 copy-start.8
  3.5 0.7 %copy-done.8 = f32[512]{0:T(512)S(1)} copy-done((f32[512]{0:T(512)S(1)}, f32[512]{0:T(512)}, u32[]{:S(2)}) %copy-start.8) | copy-done | bytes 2072
  4.2 0.0 copy-start.13
  4.2 0.0 copy-start.5
  4.2 0.0 copy-start.3
  4.2 0.0 copy-start.11
  4.2 1.4 %conv_mid.1 = (bf16[128,512]{1,0:T(8,128)(2,1)S(1)}, bf16[128,512]{1,0:T(8,128)(2,1)S(1)}, bf16[256,512]{1,0:T(8,128)(2,1)S(1)}) custom-call(bf16[768,512]{1,0:T(8,128)(2,1)S(1)} %bitcast.7, bf16[3,3,512,512]{3,2,1,0:T(8,128)(2,1)S(1)} %copy-done, f32[1,512]{1,0:T(1,128)S(1)} %bitcast.14), custom_call_target="tpu_custom_call" | custom-call | flops 2000000000 | tf_op jit(solution)/shard_map/conv_mid/pallas_call | solution.py:211
  5.6 0.0 copy-start.7
  5.6 0.0 copy-start.12
  5.6 3.7 %collective-permute-start = (bf16[128,512]{1,0:T(8,128)(2,1)S(1)}, bf16[128,512]{1,0:T(8,128)(2,1)S(1)}, u32[]{:S(2)}, u32[]{:S(2)}) collective-permute-start(bf16[128,512]{1,0:T(8,128)(2,1)S(1)} %get-tuple-element.18), channel_id=1, source_target_pairs={{0,1},{1,2},{2,3},{3,4},{4,5},{5,6},{6,7},{7,8},{8,9},{9,10},{10,1... | collective-permute-start | bytes 393224 | tf_op jit(solution)/shard_map/ppermute | solution.py:226
  9.3 1.9 %collective-permute-start.1 = (bf16[128,512]{1,0:T(8,128)(2,1)S(1)}, bf16[128,512]{1,0:T(8,128)(2,1)S(1)}, u32[]{:S(2)}, u32[]{:S(2)}) collective-permute-start(bf16[128,512]{1,0:T(8,128)(2,1)S(1)} %get-tuple-element.19), channel_id=1, source_target_pairs={{1,0},{2,1},{3,2},{4,3},{5,4},{6,5},{7,6},{8,7},{9,8},{10,9},{11,1... | collective-permute-start | bytes 393224 | tf_op jit(solution)/shard_map/ppermute | solution.py:226
  11.2 4.9 %collective-permute-start.4 = (bf16[256,512]{1,0:T(8,128)(2,1)S(1)}, bf16[256,512]{1,0:T(8,128)(2,1)S(1)}, u32[]{:S(2)}, u32[]{:S(2)}) collective-permute-start(bf16[256,512]{1,0:T(8,128)(2,1)S(1)} %get-tuple-element.22.mid_ref), channel_id=1, source_target_pairs={{0,16},{16,32},{32,48},{48,64},{64,80},{80,96},{96,112},{112,128},... | collective-permute-start | bytes 786440 | tf_op jit(solution)/shard_map/ppermute | solution.py:226
  16.1 0.0 copy-done.13
  16.1 0.1 copy.18.ids_ref
  16.2 0.0 collective-permute-done.before_ref
  16.2 0.0 collective-permute-done.1.after_ref
  16.2 0.0 copy-done.5
  16.2 0.0 copy-done.9
  16.3 0.0 copy-start.1
  16.3 2.3 %copy-done.1 = bf16[3,3,512,512]{3,2,1,0:T(8,128)(2,1)S(1)} copy-done((bf16[3,3,512,512]{3,2,1,0:T(8,128)(2,1)S(1)}, bf16[3,3,512,512]{3,2,1,0:T(8,128)(2,1)}, u32[]{:S(2)}) %copy-start.1) | copy-done | bytes 4718616
  18.6 2.6 %conv_edge.1 = (bf16[256,512]{1,0:T(8,128)(2,1)S(1)}, bf16[256,512]{1,0:T(8,128)(2,1)S(1)}) custom-call(bf16[128,512]{1,0:T(8,128)(2,1)S(1)} %collective-permute-done.before_ref, bf16[768,512]{1,0:T(8,128)(2,1)S(1)} %bitcast.8, bf16[128,512]{1,0:T(8,128)(2,1)S(1)} %collective-permute-done.1.after_ref, bf16[3,3,512,512]{3,2,1,0:T(8,128)(2,1)S(1)} %copy-done.1, ...), custom_call_target="tpu_custom_call" | custom-call | tf_op jit(solution)/shard_map/conv_edge/pallas_call | solution.py:211
  21.2 5.2 %collective-permute-start.3 = (bf16[256,512]{1,0:T(8,128)(2,1)S(1)}, bf16[256,512]{1,0:T(8,128)(2,1)S(1)}, u32[]{:S(2)}, u32[]{:S(2)}) collective-permute-start(bf16[256,512]{1,0:T(8,128)(2,1)S(1)} %get-tuple-element.21.top_ref), channel_id=1, source_target_pairs={{0,16},{16,32},{32,48},{48,64},{64,80},{80,96},{96,112},{112,128},... | collective-permute-start | bytes 786440 | tf_op jit(solution)/shard_map/ppermute | solution.py:226
  26.4 0.0 copy-done.2
  26.4 0.0 copy-done.3
  26.4 0.0 copy-done.11
  26.5 0.0 copy-done.7
  26.5 0.0 copy-done.12
  26.5 0.0 copy-start.10
  26.5 4.8 %own_part.1 = (bf16[768,512]{1,0:T(8,128)(2,1)S(1)}, f32[768,1024]{1,0:T(8,128)S(1)}) custom-call(bf16[256,512]{1,0:T(8,128)(2,1)S(1)} %get-tuple-element.21.top_ref, bf16[256,512]{1,0:T(8,128)(2,1)S(1)} %get-tuple-element.22.mid_ref, bf16[256,512]{1,0:T(8,128)(2,1)S(1)} %get-tuple-element.24.bottom_ref, bf16[512,512]{1,0:T(8,128)(2,1)S(1)} %copy-done.11, ...), custom_call_target="tpu_custom_call" | custom-call | flops 2000000000 | tf_op jit(solution)/shard_map/own_part/pallas_call | solution.py:211
  31.3 4.2 %collective-permute-start.2 = (bf16[256,512]{1,0:T(8,128)(2,1)S(1)}, bf16[256,512]{1,0:T(8,128)(2,1)S(1)}, u32[]{:S(2)}, u32[]{:S(2)}) collective-permute-start(bf16[256,512]{1,0:T(8,128)(2,1)S(1)} %get-tuple-element.24.bottom_ref), channel_id=1, source_target_pairs={{0,16},{16,32},{32,48},{48,64},{64,80},{80,96},{96,112},{112,128},... | collective-permute-start | bytes 786440 | tf_op jit(solution)/shard_map/ppermute | solution.py:226
  35.5 0.0 collective-permute-done.4.prev_ref
  35.5 0.0 copy-done.10
  35.5 2.9 %mid_rows.1.acc_in_ref = f32[768,1024]{1,0:T(8,128)S(1)} custom-call(s32[6,4]{1,0:T(8,128)S(1)} %copy.18.ids_ref, s32[6]{0:T(128)S(1)} %bitcast.16, bf16[256,512]{1,0:T(8,128)(2,1)S(1)} %collective-permute-done.4.prev_ref, bf16[768,512]{1,0:T(8,128)(2,1)S(1)} %get-tuple-element.25.q_ref, ...), custom_call_target="tpu_custom_call", output_to_operand_aliasing={{}: (4, {})} | custom-call | flops 40000000000 | tf_op jit(solution)/shard_map/mid_rows/pallas_call | solution.py:211
  38.5 0.0 copy-start.6
  38.5 4.6 %collective-permute-done.3.prev_ref = bf16[256,512]{1,0:T(8,128)(2,1)S(1)} collective-permute-done((bf16[256,512]{1,0:T(8,128)(2,1)S(1)}, bf16[256,512]{1,0:T(8,128)(2,1)S(1)}, u32[]{:S(2)}, u32[]{:S(2)}) %collective-permute-start.3) | collective-permute-done | bytes 262176 | tf_op jit(solution)/shard_map/ppermute | solution.py:226
  43.1 2.5 %collective-permute-start.6 = (bf16[256,512]{1,0:T(8,128)(2,1)S(1)}, bf16[256,512]{1,0:T(8,128)(2,1)S(1)}, u32[]{:S(2)}, u32[]{:S(2)}) collective-permute-start(bf16[256,512]{1,0:T(8,128)(2,1)S(1)} %collective-permute-done.3.prev_ref), channel_id=1, source_target_pairs={{1,0},{2,1},{3,2},{4,3},{5,4},{6,5},{7,6},{8,7},{9,8},{10,9},{11,1... | collective-permute-start | bytes 786440 | tf_op jit(solution)/shard_map/ppermute | solution.py:226
  45.5 2.5 %top_rows.1.acc_in_ref = f32[768,1024]{1,0:T(8,128)S(1)} custom-call(s32[6,4]{1,0:T(8,128)S(1)} %copy.18.ids_ref, s32[6]{0:T(128)S(1)} %bitcast.17, bf16[256,512]{1,0:T(8,128)(2,1)S(1)} %collective-permute-done.3.prev_ref, bf16[768,512]{1,0:T(8,128)(2,1)S(1)} %get-tuple-element.25.q_ref, ...), custom_call_target="tpu_custom_call", output_to_operand_aliasing={{}: (4, {})} | custom-call | flops 2000000000 | tf_op jit(solution)/shard_map/top_rows/pallas_call | solution.py:211
  48.1 0.8 %collective-permute-done.2.prev_ref = bf16[256,512]{1,0:T(8,128)(2,1)S(1)} collective-permute-done((bf16[256,512]{1,0:T(8,128)(2,1)S(1)}, bf16[256,512]{1,0:T(8,128)(2,1)S(1)}, u32[]{:S(2)}, u32[]{:S(2)}) %collective-permute-start.2) | collective-permute-done | bytes 262176 | tf_op jit(solution)/shard_map/ppermute | solution.py:226
  48.9 10.1 %collective-permute-start.5 = (bf16[256,512]{1,0:T(8,128)(2,1)S(1)}, bf16[256,512]{1,0:T(8,128)(2,1)S(1)}, u32[]{:S(2)}, u32[]{:S(2)}) collective-permute-start(bf16[256,512]{1,0:T(8,128)(2,1)S(1)} %collective-permute-done.2.prev_ref), channel_id=1, source_target_pairs={{0,1},{1,2},{2,3},{3,4},{4,5},{5,6},{6,7},{7,8},{8,9},{9,10},{10,1... | collective-permute-start | bytes 786440 | tf_op jit(solution)/shard_map/ppermute | solution.py:226
  59.0 0.0 collective-permute-done.6.below_ref
  59.0 0.0 copy-done.6
  59.0 4.3 %bottom_rows.1.rest_hbm = bf16[768,512]{1,0:T(8,128)(2,1)} custom-call(s32[6,4]{1,0:T(8,128)S(1)} %copy.18.ids_ref, s32[6]{0:T(128)S(1)} %bitcast.18, bf16[256,512]{1,0:T(8,128)(2,1)S(1)} %collective-permute-done.2.prev_ref, bf16[256,512]{1,0:T(8,128)(2,1)S(1)} %collective-permute-done.6.below_ref, bf16[768,512]{1,0:T(8,128)(2,1)S(1)} %get-tuple-element.25.q_ref, ...), custom_call_target="tpu_custom_call" | custom-call | flops 2000000000 | tf_op jit(solution)/shard_map/bottom_rows/pallas_call | solution.py:211
  63.3 0.0 collective-permute-done.5.above_ref
  63.3 2.6 %last_rows.1 = bf16[768,512]{1,0:T(8,128)(2,1)} custom-call(s32[6,4]{1,0:T(8,128)S(1)} %copy.18.ids_ref, s32[6]{0:T(128)S(1)} %bitcast.19, bf16[256,512]{1,0:T(8,128)(2,1)S(1)} %collective-permute-done.5.above_ref, bf16[768,512]{1,0:T(8,128)(2,1)S(1)} %get-tuple-element.25.q_ref, ...), custom_call_target="tpu_custom_call", output_to_operand_aliasing={{}: (10, {})} | custom-call | flops 2000000000 | tf_op jit(solution)/shard_map/last_rows/pallas_call | solution.py:211
  (2 shorter events, 0.0 us)
Async XLA Ops:
  0.0 2.3 %copy-start = (bf16[3,3,512,512]{3,2,1,0:T(8,128)(2,1)S(1)}, bf16[3,3,512,512]{3,2,1,0:T(8,128)(2,1)}, u32[]{:S(2)}) copy-start(bf16[3,3,512,512]{3,2,1,0:T(8,128)(2,1)} %w_ref.3) | copy-start | bytes 14155780
  2.3 1.1 %copy-start.4 = (bf16[1,6,128,512]{3,2,1,0:T(8,128)(2,1)S(1)}, bf16[1,6,128,512]{3,2,1,0:T(8,128)(2,1)}, u32[]{:S(2)}) copy-start(bf16[1,6,128,512]{3,2,1,0:T(8,128)(2,1)} %param.11) | copy-start | bytes 2359300
  3.5 0.7 %copy-start.8 = (f32[512]{0:T(512)S(1)}, f32[512]{0:T(512)}, u32[]{:S(2)}) copy-start(f32[512]{0:T(512)} %param.13) | copy-start | bytes 6148
  4.2 12.0 %copy-start.13 = (s32[1,6,4]{1,2,0:T(4,128)S(1)}, s32[1,6,4]{1,2,0:T(4,128)}, u32[]{:S(2)}) copy-start(s32[1,6,4]{1,2,0:T(4,128)} %param.20) | copy-start | bytes 292
  4.2 12.1 %copy-start.5 = (bf16[1,6,128,512]{3,2,1,0:T(8,128)(2,1)S(1)}, bf16[1,6,128,512]{3,2,1,0:T(8,128)(2,1)}, u32[]{:S(2)}) copy-start(bf16[1,6,128,512]{3,2,1,0:T(8,128)(2,1)} %param.11) | copy-start | bytes 2359300
  4.2 12.1 %copy-start.9 = (f32[512]{0:T(512)S(1)}, f32[512]{0:T(512)}, u32[]{:S(2)}) copy-start(f32[512]{0:T(512)} %param.13) | copy-start | bytes 6148
  4.2 22.3 %copy-start.2 = (bf16[512,512]{1,0:T(8,128)(2,1)S(1)}, bf16[512,512]{1,0:T(8,128)(2,1)}, u32[]{:S(2)}) copy-start(bf16[512,512]{1,0:T(8,128)(2,1)} %wk_ref.9) | copy-start | bytes 1572868
  4.2 22.3 %copy-start.3 = (bf16[512,512]{1,0:T(8,128)(2,1)S(1)}, bf16[512,512]{1,0:T(8,128)(2,1)}, u32[]{:S(2)}) copy-start(bf16[512,512]{1,0:T(8,128)(2,1)} %wv_ref.9) | copy-start | bytes 1572868
  4.2 22.3 %copy-start.11 = (bf16[512,512]{1,0:T(8,128)(2,1)S(1)}, bf16[512,512]{1,0:T(8,128)(2,1)}, u32[]{:S(2)}) copy-start(bf16[512,512]{1,0:T(8,128)(2,1)} %wq_ref.1) | copy-start | bytes 1572868
  5.6 20.9 %copy-start.7 = (f32[512]{0:T(512)S(1)}, f32[512]{0:T(512)}, u32[]{:S(2)}) copy-start(f32[512]{0:T(512)} %param.19) | copy-start | bytes 6148
  5.6 20.9 %copy-start.12 = (f32[512]{0:T(512)S(1)}, f32[512]{0:T(512)}, u32[]{:S(2)}) copy-start(f32[512]{0:T(512)} %param.18) | copy-start | bytes 6148
  5.6 10.6 %collective-permute-start = (bf16[128,512]{1,0:T(8,128)(2,1)S(1)}, bf16[128,512]{1,0:T(8,128)(2,1)S(1)}, u32[]{:S(2)}, u32[]{:S(2)}) collective-permute-start(bf16[128,512]{1,0:T(8,128)(2,1)S(1)} %get-tuple-element.18), channel_id=1, source_target_pairs={{0,1},{1,2},{2,3},{3,4},{4,5},{5,6},{6,7},{7,8},{8,9},{9,10},{10,1... | collective-permute-start | bytes 393224 | tf_op jit(solution)/shard_map/ppermute | solution.py:226
  9.3 6.9 %collective-permute-start.1 = (bf16[128,512]{1,0:T(8,128)(2,1)S(1)}, bf16[128,512]{1,0:T(8,128)(2,1)S(1)}, u32[]{:S(2)}, u32[]{:S(2)}) collective-permute-start(bf16[128,512]{1,0:T(8,128)(2,1)S(1)} %get-tuple-element.19), channel_id=1, source_target_pairs={{1,0},{2,1},{3,2},{4,3},{5,4},{6,5},{7,6},{8,7},{9,8},{10,9},{11,1... | collective-permute-start | bytes 393224 | tf_op jit(solution)/shard_map/ppermute | solution.py:226
  11.2 24.3 %collective-permute-start.4 = (bf16[256,512]{1,0:T(8,128)(2,1)S(1)}, bf16[256,512]{1,0:T(8,128)(2,1)S(1)}, u32[]{:S(2)}, u32[]{:S(2)}) collective-permute-start(bf16[256,512]{1,0:T(8,128)(2,1)S(1)} %get-tuple-element.22.mid_ref), channel_id=1, source_target_pairs={{0,16},{16,32},{32,48},{48,64},{64,80},{80,96},{96,112},{112,128},... | collective-permute-start | bytes 786440 | tf_op jit(solution)/shard_map/ppermute | solution.py:226
  16.3 2.3 %copy-start.1 = (bf16[3,3,512,512]{3,2,1,0:T(8,128)(2,1)S(1)}, bf16[3,3,512,512]{3,2,1,0:T(8,128)(2,1)}, u32[]{:S(2)}) copy-start(bf16[3,3,512,512]{3,2,1,0:T(8,128)(2,1)} %w_ref.3) | copy-start | bytes 14155780
  21.2 21.8 %collective-permute-start.3 = (bf16[256,512]{1,0:T(8,128)(2,1)S(1)}, bf16[256,512]{1,0:T(8,128)(2,1)S(1)}, u32[]{:S(2)}, u32[]{:S(2)}) collective-permute-start(bf16[256,512]{1,0:T(8,128)(2,1)S(1)} %get-tuple-element.21.top_ref), channel_id=1, source_target_pairs={{0,16},{16,32},{32,48},{48,64},{64,80},{80,96},{96,112},{112,128},... | collective-permute-start | bytes 786440 | tf_op jit(solution)/shard_map/ppermute | solution.py:226
  26.5 9.1 %copy-start.10 = (s32[1,6]{1,0:T(1,128)S(1)}, s32[1,6]{1,0:T(1,128)}, u32[]{:S(2)}) copy-start(s32[1,6]{1,0:T(1,128)} %param.21) | copy-start | bytes 76
  31.3 17.6 %collective-permute-start.2 = (bf16[256,512]{1,0:T(8,128)(2,1)S(1)}, bf16[256,512]{1,0:T(8,128)(2,1)S(1)}, u32[]{:S(2)}, u32[]{:S(2)}) collective-permute-start(bf16[256,512]{1,0:T(8,128)(2,1)S(1)} %get-tuple-element.24.bottom_ref), channel_id=1, source_target_pairs={{0,16},{16,32},{32,48},{48,64},{64,80},{80,96},{96,112},{112,128},... | collective-permute-start | bytes 786440 | tf_op jit(solution)/shard_map/ppermute | solution.py:226
  38.5 20.6 %copy-start.6 = (bf16[512,512]{1,0:T(8,128)(2,1)S(1)}, bf16[512,512]{1,0:T(8,128)(2,1)}, u32[]{:S(2)}) copy-start(bf16[512,512]{1,0:T(8,128)(2,1)} %wo_ref.3) | copy-start | bytes 1572868
  43.1 16.0 %collective-permute-start.6 = (bf16[256,512]{1,0:T(8,128)(2,1)S(1)}, bf16[256,512]{1,0:T(8,128)(2,1)S(1)}, u32[]{:S(2)}, u32[]{:S(2)}) collective-permute-start(bf16[256,512]{1,0:T(8,128)(2,1)S(1)} %collective-permute-done.3.prev_ref), channel_id=1, source_target_pairs={{1,0},{2,1},{3,2},{4,3},{5,4},{6,5},{7,6},{8,7},{9,8},{10,9},{11,1... | collective-permute-start | bytes 786440 | tf_op jit(solution)/shard_map/ppermute | solution.py:226
  48.9 14.4 %collective-permute-start.5 = (bf16[256,512]{1,0:T(8,128)(2,1)S(1)}, bf16[256,512]{1,0:T(8,128)(2,1)S(1)}, u32[]{:S(2)}, u32[]{:S(2)}) collective-permute-start(bf16[256,512]{1,0:T(8,128)(2,1)S(1)} %collective-permute-done.2.prev_ref), channel_id=1, source_target_pairs={{0,1},{1,2},{2,3},{3,4},{4,5},{5,6},{6,7},{7,8},{8,9},{9,10},{10,1... | collective-permute-start | bytes 786440 | tf_op jit(solution)/shard_map/ppermute | solution.py:226

commit v4 on v3

--- a/solution.py
+++ b/solution.py
@@ -38,11 +38,59 @@
     return (from_left(left) + (mid + b_ref[...]) + from_right(right)).astype(jnp.bfloat16)
 
 
-def conv_mid_kernel(x_ref, w_ref, b_ref, first_ref, last_ref, mid_ref):
+def weight_copies(w_hbm, w_ref, sems):
+    return [
+        [pltpu.make_async_copy(w_hbm.at[a, c], w_ref.at[a, c], sems.at[a, c]) for a in range(3)]
+        for c in (1, 0, 2)
+    ]
+
+
+def start(copies):
+    for copy in copies:
+        copy.start()
+
+
+def wait(copies):
+    for copy in copies:
+        copy.wait()
+
+
+def column_sum(lines, w_ref, c):
+    return sum(dot(lines(a), w_ref[a, c]) for a in range(3))
+
+
+def streamed_columns(lines, w_hbm, w_ref, sems, ready):
+    mid, left, right = weight_copies(w_hbm, w_ref, sems)
+    start(mid)
+    ready()
+    start(left)
+    wait(mid)
+    y_mid = column_sum(lines, w_ref, 1)
+    start(right)
+    wait(left)
+    y_left = column_sum(lines, w_ref, 0)
+    wait(right)
+    return y_left, y_mid, column_sum(lines, w_ref, 2)
+
+
+def conv_mid_kernel(x_hbm, w_hbm, b_hbm, first_ref, last_ref, mid_ref, x_ref, w_ref, b_ref, sems, x_sems):
     rows = mid_ref.shape[0] // BLOCK
-    first_ref[...] = x_ref[row_of(0)]
-    last_ref[...] = x_ref[row_of(rows + 2 * DISP - 1)]
-    mid_ref[...] = convolved(lambda a: x_ref[row_of(DISP - 1 + a, rows)], w_ref, b_ref)
+    inputs = [
+        pltpu.make_async_copy(x_hbm, x_ref, x_sems.at[0]),
+        pltpu.make_async_copy(b_hbm, b_ref, x_sems.at[1]),
+    ]
+
+    def ready():
+        wait(inputs)
+        first_ref[...] = x_ref[row_of(0)]
+        last_ref[...] = x_ref[row_of(rows + 2 * DISP - 1)]
+
+    def lines(a):
+        return x_ref[row_of(DISP - 1 + a, rows)]
+
+    start(inputs)
+    left, mid, right = streamed_columns(lines, w_hbm, w_ref, sems, ready)
+    mid_ref[...] = (from_left(left) + (mid + b_ref[...]) + from_right(right)).astype(jnp.bfloat16)
 
 
 def conv_edge_kernel(before_ref, x_ref, after_ref, w_ref, b_ref, top_ref, bottom_ref):
@@ -111,7 +159,18 @@
             )
 
 
-def absorb(ids_ref, counts_ref, pieces, q_ref, acc_ref, wk_ref, wv_ref, gk_ref, k_ref, v_ref, base=0):
+def spans_of(fresh, low, high):
+    spans = []
+    for row in range(low, high):
+        if spans and spans[-1][2] == fresh[row]:
+            spans[-1] = (spans[-1][0], spans[-1][1] + 1, fresh[row])
+        else:
+            spans.append((row, 1, fresh[row]))
+    return spans
+
+
+def absorb(ids_ref, counts_ref, pieces, q_ref, acc_in_ref, acc_ref, wk_ref, wv_ref, gk_ref, k_ref, v_ref, base=0):
+    fresh = [True] * (acc_ref.shape[0] // BLOCK)
     rows = q_ref.shape[0] // BLOCK
     has_previous = lax.axis_index("frame") > 0
     first_row = lax.axis_index("row") * rows
@@ -130,38 +189,54 @@
                     times += jnp.where(named, jnp.float32(1), jnp.float32(0))
                 weights.append(times)
             queries = row_of(low, high + 1 - low)
-            sums = row_of(low - base, high + 1 - low)
+            spans = spans_of(fresh, low - base, high + 1 - base)
             source = row_of(done + i)
             for p in range(HEADS // 2):
                 cols = pl.ds(p * PAIR, PAIR)
-                acc_ref[sums, pl.ds(2 * p * PAIR, 2 * PAIR)] += pair_product(
+                both = pair_product(
                     q_ref[queries, cols], k_ref[source, cols], v_ref[source, cols], weights
                 )
+                both_cols = pl.ds(2 * p * PAIR, 2 * PAIR)
+                begin = 0
+                for row, count, first_time in spans:
+                    so_far = acc_in_ref if first_time else acc_ref
+                    stop = begin + count * BLOCK
+                    here = row_of(row, count)
+                    acc_ref[here, both_cols] = (
+                        so_far[row_of(row + base, count), both_cols] if first_time
+                        else so_far[here, both_cols]
+                    ) + both[begin:stop]
+                    begin = stop
+            for row in range(low - base, high + 1 - base):
+                fresh[row] = False
         done += len(places)
+    for row, waiting in enumerate(fresh):
+        if waiting:
+            acc_ref[row_of(row)] = acc_in_ref[row_of(row + base)]
 
 
 def mid_kernel(
     ids_ref, counts_ref, prev_ref, q_ref, acc_in_ref, wk_ref, wv_ref, gk_ref, acc_ref, k_ref, v_ref
 ):
     rows = q_ref.shape[0] // BLOCK
-    acc_ref[...] = acc_in_ref[...]
     pieces = ((prev_ref, tuple(range(DISP, rows - DISP))),)
-    absorb(ids_ref, counts_ref, pieces, q_ref, acc_ref, wk_ref, wv_ref, gk_ref, k_ref, v_ref)
+    absorb(ids_ref, counts_ref, pieces, q_ref, acc_in_ref, acc_ref, wk_ref, wv_ref, gk_ref, k_ref, v_ref)
 
 
 def top_kernel(
     ids_ref, counts_ref, prev_ref, q_ref, acc_in_ref, wk_ref, wv_ref, gk_ref, acc_ref, k_ref, v_ref
 ):
-    acc_ref[...] = acc_in_ref[...]
     pieces = ((prev_ref, tuple(range(DISP))),)
-    absorb(ids_ref, counts_ref, pieces, q_ref, acc_ref, wk_ref, wv_ref, gk_ref, k_ref, v_ref)
+    absorb(ids_ref, counts_ref, pieces, q_ref, acc_in_ref, acc_ref, wk_ref, wv_ref, gk_ref, k_ref, v_ref)
 
 
 def finish(acc_ref, wo_ref, pieces, out_ref):
     parts = []
     for p in range(HEADS // 2):
         both = acc_ref[:, pl.ds(2 * p * PAIR, 2 * PAIR)]
-        parts.append((both[:, :PAIR] / both[:, PAIR:]).astype(jnp.bfloat16))
+        norm = both[:, PAIR:]
+        guess = pl.reciprocal(norm, approx=True)
+        parts.append((both[:, :PAIR] * (guess * (2.0 - norm * guess))).astype(jnp.bfloat16))
     change = dot(jnp.concatenate(parts, 1), wo_ref[...])
     begin = 0
     for ref in pieces:
@@ -176,9 +251,8 @@
     mid_ref, bottom_ref, wo_ref, out_hbm, acc_ref, k_ref, v_ref, out_ref, sem,
 ):
     rows = q_ref.shape[0] // BLOCK
-    acc_ref[...] = acc_in_ref[DISP * BLOCK :]
     pieces = ((prev_ref, tuple(range(rows - DISP, rows))), (below_ref, tuple(range(rows, rows + DISP))))
-    absorb(ids_ref, counts_ref, pieces, q_ref, acc_ref, wk_ref, wv_ref, gk_ref, k_ref, v_ref, DISP)
+    absorb(ids_ref, counts_ref, pieces, q_ref, acc_in_ref, acc_ref, wk_ref, wv_ref, gk_ref, k_ref, v_ref, DISP)
     finish(acc_ref, wo_ref, (mid_ref, bottom_ref), out_ref)
     copy = pltpu.make_async_copy(out_ref, out_hbm.at[row_of(DISP, rows - DISP)], sem)
     copy.start()
@@ -190,9 +264,8 @@
     top_ref, wo_ref, rest_hbm, out_hbm, acc_ref, k_ref, v_ref, out_ref, sem,
 ):
     del rest_hbm
-    acc_ref[...] = acc_in_ref[: DISP * BLOCK]
     pieces = ((above_ref, tuple(range(-DISP, 0))),)
-    absorb(ids_ref, counts_ref, pieces, q_ref, acc_ref, wk_ref, wv_ref, gk_ref, k_ref, v_ref)
+    absorb(ids_ref, counts_ref, pieces, q_ref, acc_in_ref, acc_ref, wk_ref, wv_ref, gk_ref, k_ref, v_ref)
     finish(acc_ref, wo_ref, (top_ref,), out_ref)
     copy = pltpu.make_async_copy(out_ref, out_hbm.at[row_of(0, DISP)], sem)
     copy.start()
@@ -244,7 +317,11 @@
     first, last, mid = call(
         conv_mid_kernel, "conv_mid", (x, conv_weight, bias),
         [((BLOCK, chans), half), ((BLOCK, chans), half), ((tokens - 2 * reach, chans), half)],
-        cost=2,
+        [
+            pltpu.VMEM((tokens, chans), half), pltpu.VMEM(conv_weight.shape, half),
+            pltpu.VMEM(bias.shape, full), dma((3, 3)), dma((2,)),
+        ],
+        [HBM, HBM, HBM], limit=58, cost=2,
     )
     before = passed_on(last, "row", 1)
     after = passed_on(first, "row", -1)

time: 66.5 us -> 65.9 us (level)
  local copies, waits for them, and re-layouts: 6.62 us -> 2.48 us
  Pallas kernels: 21.1 us -> 24.6 us
  waiting for transfers between devices: 5.45 us -> 6.46 us
  starting transfers between devices: 32.5 us -> 31.5 us
    unnamed x28 -> x24, local copies, waits for them, and re-layouts: 6.53 us -> 2.38 us
    pallas_call x7, Pallas kernels: 21.1 us -> 24.6 us  [call(): pl.pallas_call(kernel, in_specs=specs or [VMEM] * len(args), out_specs=ou...]
    ppermute x7, waiting for transfers between devices: 5.45 us -> 6.46 us  [passed_on(): lax.ppermute(array, axis, [(i, i + distance) for i in devices if i + dist...]
    ppermute x7, starting transfers between devices: 32.5 us -> 31.5 us  [passed_on(): lax.ppermute(array, axis, [(i, i + distance) for i in devices if i + dist...]
where the time goes in v4:
time: 65.9 us; the launch traced here: 65.5 us
  starting transfers between devices  31.5 us (48%)
  Pallas kernels  24.6 us (37%)
  waiting for transfers between devices  6.46 us (10%)
  local copies, waits for them, and re-layouts  2.48 us (4%)
    ppermute x7, starting transfers between devices, passed_on(): lax.ppermute(array, axis, [(i, i + distance) for i in devices if i + dist...  31.5 us
    pallas_call x7, Pallas kernels, call(): pl.pallas_call(kernel, in_specs=specs or [VMEM] * len(args), out_specs=ou...  24.6 us
    ppermute x7, waiting for transfers between devices, passed_on(): lax.ppermute(array, axis, [(i, i + distance) for i in devices if i + dist...  6.46 us
    unnamed x24, local copies, waits for them, and re-layouts  2.38 us
  transfers between devices with their start and end apart: 7, of which 2 were waited for; matrix products, arithmetic and copies ran while one was open for 0% of the time, Pallas kernels for 26%

profile of v4, /device:TPU:57, one launch (start us, length us, event | category | flops | bytes accessed | tf_op | source)
XLA Modules:
  0.0 65.5 jit_solution(1891771594911660969)
XLA Ops:
  0.0 0.0 copy-start.11
  0.0 0.0 copy-start.3
  0.0 0.0 copy-start.6
  0.0 0.0 copy-start.1
  0.0 0.0 copy-start.2
  0.0 0.0 copy-start.8
  0.0 4.9 %conv_mid.1 = (bf16[128,512]{1,0:T(8,128)(2,1)}, bf16[128,512]{1,0:T(8,128)(2,1)}, bf16[256,512]{1,0:T(8,128)(2,1)}) custom-call(bf16[768,512]{1,0:T(8,128)(2,1)} %bitcast.7, bf16[3,3,512,512]{3,2,1,0:T(8,128)(2,1)} %w_ref.1, f32[1,512]{1,0:T(1,128)} %bitcast.14), custom_call_target="tpu_custom_call" | custom-call | flops 2000000000 | tf_op jit(solution)/shard_map/conv_mid/pallas_call | solution.py:284
  5.0 0.0 copy-start.5
  5.0 0.0 copy-start.10
  5.0 3.7 %collective-permute-start = (bf16[128,512]{1,0:T(8,128)(2,1)}, bf16[128,512]{1,0:T(8,128)(2,1)S(1)}, u32[]{:S(2)}, u32[]{:S(2)}) collective-permute-start(bf16[128,512]{1,0:T(8,128)(2,1)} %get-tuple-element.18), channel_id=1, source_target_pairs={{0,1},{1,2},{2,3},{3,4},{4,5},{5,6},{6,7},{7,8},{8,9},{9,10},{10,1... | collective-permute-start | bytes 393224 | tf_op jit(solution)/shard_map/ppermute | solution.py:299
  8.7 1.9 %collective-permute-start.1 = (bf16[128,512]{1,0:T(8,128)(2,1)}, bf16[128,512]{1,0:T(8,128)(2,1)S(1)}, u32[]{:S(2)}, u32[]{:S(2)}) collective-permute-start(bf16[128,512]{1,0:T(8,128)(2,1)} %get-tuple-element.19), channel_id=1, source_target_pairs={{1,0},{2,1},{3,2},{4,3},{5,4},{6,5},{7,6},{8,7},{9,8},{10,9},{11,1... | collective-permute-start | bytes 393224 | tf_op jit(solution)/shard_map/ppermute | solution.py:299
  10.6 4.9 %collective-permute-start.4 = (bf16[256,512]{1,0:T(8,128)(2,1)}, bf16[256,512]{1,0:T(8,128)(2,1)S(1)}, u32[]{:S(2)}, u32[]{:S(2)}) collective-permute-start(bf16[256,512]{1,0:T(8,128)(2,1)} %get-tuple-element.22.mid_ref), channel_id=1, source_target_pairs={{0,16},{16,32},{32,48},{48,64},{64,80},{80,96},{96,112},{112,128},... | collective-permute-start | bytes 786440 | tf_op jit(solution)/shard_map/ppermute | solution.py:299
  15.5 0.0 copy-done.11
  15.5 0.1 copy.18.ids_ref
  15.6 0.0 collective-permute-done.before_ref
  15.6 0.0 collective-permute-done.1.after_ref
  15.6 0.0 copy-done.3
  15.6 0.0 copy-done.6
  15.7 0.0 copy-start
  15.7 2.3 %copy-done = bf16[3,3,512,512]{3,2,1,0:T(8,128)(2,1)S(1)} copy-done((bf16[3,3,512,512]{3,2,1,0:T(8,128)(2,1)S(1)}, bf16[3,3,512,512]{3,2,1,0:T(8,128)(2,1)}, u32[]{:S(2)}) %copy-start) | copy-done | bytes 4718616
  18.0 0.0 copy-start.9
  18.0 2.6 %conv_edge.1 = (bf16[256,512]{1,0:T(8,128)(2,1)S(1)}, bf16[256,512]{1,0:T(8,128)(2,1)S(1)}) custom-call(bf16[128,512]{1,0:T(8,128)(2,1)S(1)} %collective-permute-done.before_ref, bf16[768,512]{1,0:T(8,128)(2,1)S(1)} %bitcast.8, bf16[128,512]{1,0:T(8,128)(2,1)S(1)} %collective-permute-done.1.after_ref, bf16[3,3,512,512]{3,2,1,0:T(8,128)(2,1)S(1)} %copy-done, ...), custom_call_target="tpu_custom_call" | custom-call | tf_op jit(solution)/shard_map/conv_edge/pallas_call | solution.py:284
  20.6 5.2 %collective-permute-start.3 = (bf16[256,512]{1,0:T(8,128)(2,1)S(1)}, bf16[256,512]{1,0:T(8,128)(2,1)S(1)}, u32[]{:S(2)}, u32[]{:S(2)}) collective-permute-start(bf16[256,512]{1,0:T(8,128)(2,1)S(1)} %get-tuple-element.21.top_ref), channel_id=1, source_target_pairs={{0,16},{16,32},{32,48},{48,64},{64,80},{80,96},{96,112},{112,128},... | collective-permute-start | bytes 786440 | tf_op jit(solution)/shard_map/ppermute | solution.py:299
  25.8 0.0 copy-done.1
  25.8 0.0 copy-done.2
  25.8 0.0 copy-done.8
  25.9 0.0 copy-done.5
  25.9 0.0 copy-done.10
  25.9 0.0 copy-done.9
  25.9 0.0 copy-start.7
  25.9 4.8 %own_part.1 = (bf16[768,512]{1,0:T(8,128)(2,1)S(1)}, f32[768,1024]{1,0:T(8,128)S(1)}) custom-call(bf16[256,512]{1,0:T(8,128)(2,1)S(1)} %get-tuple-element.21.top_ref, bf16[256,512]{1,0:T(8,128)(2,1)S(1)} %copy-done.9, bf16[256,512]{1,0:T(8,128)(2,1)S(1)} %get-tuple-element.24.bottom_ref, bf16[512,512]{1,0:T(8,128)(2,1)S(1)} %copy-done.8, ...), custom_call_target="tpu_custom_call" | custom-call | flops 2000000000 | tf_op jit(solution)/shard_map/own_part/pallas_call | solution.py:284
  30.7 4.4 %collective-permute-start.2 = (bf16[256,512]{1,0:T(8,128)(2,1)S(1)}, bf16[256,512]{1,0:T(8,128)(2,1)S(1)}, u32[]{:S(2)}, u32[]{:S(2)}) collective-permute-start(bf16[256,512]{1,0:T(8,128)(2,1)S(1)} %get-tuple-element.24.bottom_ref), channel_id=1, source_target_pairs={{0,16},{16,32},{32,48},{48,64},{64,80},{80,96},{96,112},{112,128},... | collective-permute-start | bytes 786440 | tf_op jit(solution)/shard_map/ppermute | solution.py:299
  35.1 0.0 collective-permute-done.4.prev_ref
  35.1 0.0 copy-done.7
  35.2 2.9 %mid_rows.1.acc_in_ref = f32[768,1024]{1,0:T(8,128)S(1)} custom-call(s32[6,4]{1,0:T(8,128)S(1)} %copy.18.ids_ref, s32[6]{0:T(128)S(1)} %bitcast.16, bf16[256,512]{1,0:T(8,128)(2,1)S(1)} %collective-permute-done.4.prev_ref, bf16[768,512]{1,0:T(8,128)(2,1)S(1)} %get-tuple-element.25.q_ref, ...), custom_call_target="tpu_custom_call", output_to_operand_aliasing={{}: (4, {})} | custom-call | flops 40000000000 | tf_op jit(solution)/shard_map/mid_rows/pallas_call | solution.py:284
  38.1 0.0 copy-start.4
  38.1 4.4 %collective-permute-done.3.prev_ref = bf16[256,512]{1,0:T(8,128)(2,1)S(1)} collective-permute-done((bf16[256,512]{1,0:T(8,128)(2,1)S(1)}, bf16[256,512]{1,0:T(8,128)(2,1)S(1)}, u32[]{:S(2)}, u32[]{:S(2)}) %collective-permute-start.3) | collective-permute-done | bytes 262176 | tf_op jit(solution)/shard_map/ppermute | solution.py:299
  42.5 2.5 %collective-permute-start.6 = (bf16[256,512]{1,0:T(8,128)(2,1)S(1)}, bf16[256,512]{1,0:T(8,128)(2,1)S(1)}, u32[]{:S(2)}, u32[]{:S(2)}) collective-permute-start(bf16[256,512]{1,0:T(8,128)(2,1)S(1)} %collective-permute-done.3.prev_ref), channel_id=1, source_target_pairs={{1,0},{2,1},{3,2},{4,3},{5,4},{6,5},{7,6},{8,7},{9,8},{10,9},{11,1... | collective-permute-start | bytes 786440 | tf_op jit(solution)/shard_map/ppermute | solution.py:299
  44.9 2.5 %top_rows.1.acc_in_ref = f32[768,1024]{1,0:T(8,128)S(1)} custom-call(s32[6,4]{1,0:T(8,128)S(1)} %copy.18.ids_ref, s32[6]{0:T(128)S(1)} %bitcast.17, bf16[256,512]{1,0:T(8,128)(2,1)S(1)} %collective-permute-done.3.prev_ref, bf16[768,512]{1,0:T(8,128)(2,1)S(1)} %get-tuple-element.25.q_ref, ...), custom_call_target="tpu_custom_call", output_to_operand_aliasing={{}: (4, {})} | custom-call | flops 2000000000 | tf_op jit(solution)/shard_map/top_rows/pallas_call | solution.py:284
  47.5 2.0 %collective-permute-done.2.prev_ref = bf16[256,512]{1,0:T(8,128)(2,1)S(1)} collective-permute-done((bf16[256,512]{1,0:T(8,128)(2,1)S(1)}, bf16[256,512]{1,0:T(8,128)(2,1)S(1)}, u32[]{:S(2)}, u32[]{:S(2)}) %collective-permute-start.2) | collective-permute-done | bytes 262176 | tf_op jit(solution)/shard_map/ppermute | solution.py:299
  49.5 8.9 %collective-permute-start.5 = (bf16[256,512]{1,0:T(8,128)(2,1)S(1)}, bf16[256,512]{1,0:T(8,128)(2,1)S(1)}, u32[]{:S(2)}, u32[]{:S(2)}) collective-permute-start(bf16[256,512]{1,0:T(8,128)(2,1)S(1)} %collective-permute-done.2.prev_ref), channel_id=1, source_target_pairs={{0,1},{1,2},{2,3},{3,4},{4,5},{5,6},{6,7},{7,8},{8,9},{9,10},{10,1... | collective-permute-start | bytes 786440 | tf_op jit(solution)/shard_map/ppermute | solution.py:299
  58.4 0.0 collective-permute-done.6.below_ref
  58.5 0.0 copy-done.4
  58.5 4.3 %bottom_rows.1.rest_hbm = bf16[768,512]{1,0:T(8,128)(2,1)} custom-call(s32[6,4]{1,0:T(8,128)S(1)} %copy.18.ids_ref, s32[6]{0:T(128)S(1)} %bitcast.18, bf16[256,512]{1,0:T(8,128)(2,1)S(1)} %collective-permute-done.2.prev_ref, bf16[256,512]{1,0:T(8,128)(2,1)S(1)} %collective-permute-done.6.below_ref, bf16[768,512]{1,0:T(8,128)(2,1)S(1)} %get-tuple-element.25.q_ref, ...), custom_call_target="tpu_custom_call" | custom-call | flops 2000000000 | tf_op jit(solution)/shard_map/bottom_rows/pallas_call | solution.py:284
  62.7 0.0 collective-permute-done.5.above_ref
  62.8 2.6 %last_rows.1 = bf16[768,512]{1,0:T(8,128)(2,1)} custom-call(s32[6,4]{1,0:T(8,128)S(1)} %copy.18.ids_ref, s32[6]{0:T(128)S(1)} %bitcast.19, bf16[256,512]{1,0:T(8,128)(2,1)S(1)} %collective-permute-done.5.above_ref, bf16[768,512]{1,0:T(8,128)(2,1)S(1)} %get-tuple-element.25.q_ref, ...), custom_call_target="tpu_custom_call", output_to_operand_aliasing={{}: (10, {})} | custom-call | flops 2000000000 | tf_op jit(solution)/shard_map/last_rows/pallas_call | solution.py:284
Async XLA Ops:
  0.0 15.5 %copy-start.11 = (s32[1,6,4]{1,2,0:T(4,128)S(1)}, s32[1,6,4]{1,2,0:T(4,128)}, u32[]{:S(2)}) copy-start(s32[1,6,4]{1,2,0:T(4,128)} %param.20) | copy-start | bytes 292
  0.0 15.6 %copy-start.3 = (bf16[1,6,128,512]{3,2,1,0:T(8,128)(2,1)S(1)}, bf16[1,6,128,512]{3,2,1,0:T(8,128)(2,1)}, u32[]{:S(2)}) copy-start(bf16[1,6,128,512]{3,2,1,0:T(8,128)(2,1)} %param.11) | copy-start | bytes 2359300
  0.0 15.6 %copy-start.6 = (f32[512]{0:T(512)S(1)}, f32[512]{0:T(512)}, u32[]{:S(2)}) copy-start(f32[512]{0:T(512)} %param.13) | copy-start | bytes 6148
  0.0 25.8 %copy-start.1 = (bf16[512,512]{1,0:T(8,128)(2,1)S(1)}, bf16[512,512]{1,0:T(8,128)(2,1)}, u32[]{:S(2)}) copy-start(bf16[512,512]{1,0:T(8,128)(2,1)} %wk_ref.9) | copy-start | bytes 1572868
  0.0 25.8 %copy-start.2 = (bf16[512,512]{1,0:T(8,128)(2,1)S(1)}, bf16[512,512]{1,0:T(8,128)(2,1)}, u32[]{:S(2)}) copy-start(bf16[512,512]{1,0:T(8,128)(2,1)} %wv_ref.9) | copy-start | bytes 1572868
  0.0 25.8 %copy-start.8 = (bf16[512,512]{1,0:T(8,128)(2,1)S(1)}, bf16[512,512]{1,0:T(8,128)(2,1)}, u32[]{:S(2)}) copy-start(bf16[512,512]{1,0:T(8,128)(2,1)} %wq_ref.1) | copy-start | bytes 1572868
  5.0 20.9 %copy-start.5 = (f32[512]{0:T(512)S(1)}, f32[512]{0:T(512)}, u32[]{:S(2)}) copy-start(f32[512]{0:T(512)} %param.19) | copy-start | bytes 6148
  5.0 20.9 %copy-start.10 = (f32[512]{0:T(512)S(1)}, f32[512]{0:T(512)}, u32[]{:S(2)}) copy-start(f32[512]{0:T(512)} %param.18) | copy-start | bytes 6148
  5.0 10.6 %collective-permute-start = (bf16[128,512]{1,0:T(8,128)(2,1)}, bf16[128,512]{1,0:T(8,128)(2,1)S(1)}, u32[]{:S(2)}, u32[]{:S(2)}) collective-permute-start(bf16[128,512]{1,0:T(8,128)(2,1)} %get-tuple-element.18), channel_id=1, source_target_pairs={{0,1},{1,2},{2,3},{3,4},{4,5},{5,6},{6,7},{7,8},{8,9},{9,10},{10,1... | collective-permute-start | bytes 393224 | tf_op jit(solution)/shard_map/ppermute | solution.py:299
  8.7 6.9 %collective-permute-start.1 = (bf16[128,512]{1,0:T(8,128)(2,1)}, bf16[128,512]{1,0:T(8,128)(2,1)S(1)}, u32[]{:S(2)}, u32[]{:S(2)}) collective-permute-start(bf16[128,512]{1,0:T(8,128)(2,1)} %get-tuple-element.19), channel_id=1, source_target_pairs={{1,0},{2,1},{3,2},{4,3},{5,4},{6,5},{7,6},{8,7},{9,8},{10,9},{11,1... | collective-permute-start | bytes 393224 | tf_op jit(solution)/shard_map/ppermute | solution.py:299
  10.6 24.5 %collective-permute-start.4 = (bf16[256,512]{1,0:T(8,128)(2,1)}, bf16[256,512]{1,0:T(8,128)(2,1)S(1)}, u32[]{:S(2)}, u32[]{:S(2)}) collective-permute-start(bf16[256,512]{1,0:T(8,128)(2,1)} %get-tuple-element.22.mid_ref), channel_id=1, source_target_pairs={{0,16},{16,32},{32,48},{48,64},{64,80},{80,96},{96,112},{112,128},... | collective-permute-start | bytes 786440 | tf_op jit(solution)/shard_map/ppermute | solution.py:299
  15.7 2.3 %copy-start = (bf16[3,3,512,512]{3,2,1,0:T(8,128)(2,1)S(1)}, bf16[3,3,512,512]{3,2,1,0:T(8,128)(2,1)}, u32[]{:S(2)}) copy-start(bf16[3,3,512,512]{3,2,1,0:T(8,128)(2,1)} %w_ref.1) | copy-start | bytes 14155780
  18.0 7.9 %copy-start.9 = (bf16[256,512]{1,0:T(8,128)(2,1)S(1)}, bf16[256,512]{1,0:T(8,128)(2,1)}, u32[]{:S(2)}) copy-start(bf16[256,512]{1,0:T(8,128)(2,1)} %get-tuple-element.22.mid_ref) | copy-start | bytes 786436
  20.6 21.9 %collective-permute-start.3 = (bf16[256,512]{1,0:T(8,128)(2,1)S(1)}, bf16[256,512]{1,0:T(8,128)(2,1)S(1)}, u32[]{:S(2)}, u32[]{:S(2)}) collective-permute-start(bf16[256,512]{1,0:T(8,128)(2,1)S(1)} %get-tuple-element.21.top_ref), channel_id=1, source_target_pairs={{0,16},{16,32},{32,48},{48,64},{64,80},{80,96},{96,112},{112,128},... | collective-permute-start | bytes 786440 | tf_op jit(solution)/shard_map/ppermute | solution.py:299
  25.9 9.3 %copy-start.7 = (s32[1,6]{1,0:T(1,128)S(1)}, s32[1,6]{1,0:T(1,128)}, u32[]{:S(2)}) copy-start(s32[1,6]{1,0:T(1,128)} %param.21) | copy-start | bytes 76
  30.7 18.8 %collective-permute-start.2 = (bf16[256,512]{1,0:T(8,128)(2,1)S(1)}, bf16[256,512]{1,0:T(8,128)(2,1)S(1)}, u32[]{:S(2)}, u32[]{:S(2)}) collective-permute-start(bf16[256,512]{1,0:T(8,128)(2,1)S(1)} %get-tuple-element.24.bottom_ref), channel_id=1, source_target_pairs={{0,16},{16,32},{32,48},{48,64},{64,80},{80,96},{96,112},{112,128},... | collective-permute-start | bytes 786440 | tf_op jit(solution)/shard_map/ppermute | solution.py:299
  38.1 20.4 %copy-start.4 = (bf16[512,512]{1,0:T(8,128)(2,1)S(1)}, bf16[512,512]{1,0:T(8,128)(2,1)}, u32[]{:S(2)}) copy-start(bf16[512,512]{1,0:T(8,128)(2,1)} %wo_ref.3) | copy-start | bytes 1572868
  42.5 16.0 %collective-permute-start.6 = (bf16[256,512]{1,0:T(8,128)(2,1)S(1)}, bf16[256,512]{1,0:T(8,128)(2,1)S(1)}, u32[]{:S(2)}, u32[]{:S(2)}) collective-permute-start(bf16[256,512]{1,0:T(8,128)(2,1)S(1)} %collective-permute-done.3.prev_ref), channel_id=1, source_target_pairs={{1,0},{2,1},{3,2},{4,3},{5,4},{6,5},{7,6},{8,7},{9,8},{10,9},{11,1... | collective-permute-start | bytes 786440 | tf_op jit(solution)/shard_map/ppermute | solution.py:299
  49.5 13.2 %collective-permute-start.5 = (bf16[256,512]{1,0:T(8,128)(2,1)S(1)}, bf16[256,512]{1,0:T(8,128)(2,1)S(1)}, u32[]{:S(2)}, u32[]{:S(2)}) collective-permute-start(bf16[256,512]{1,0:T(8,128)(2,1)S(1)} %collective-permute-done.2.prev_ref), channel_id=1, source_target_pairs={{0,1},{1,2},{2,3},{3,4},{4,5},{5,6},{6,7},{7,8},{8,9},{9,10},{10,1... | collective-permute-start | bytes 786440 | tf_op jit(solution)/shard_map/ppermute | solution.py:299
